TPU v7x, 32 devices: a whole 2x2x4 slice. The times are simulated.
32 devices in a mesh: dp: 8 (over z, y), fsdp: 4 (over x, core).
Axes of the slice: x: 2, y: 2, z: 4, core: 2. Of those that a mesh axis runs over, the one named last changes fastest.
Arguments:
- tokens: bfloat16 [4096, 1024], P(('dp', 'fsdp')), may hold values from -6 to 6
- cotangent: bfloat16 [4096, 1024], P(('dp', 'fsdp')), may hold values from -6 to 6
- tile_len: int32 [128], P(('dp', 'fsdp')), may hold values from 0 to 32, as said below
- tile_join: int32 [128], P(('dp', 'fsdp')), may hold values from 0 to 1, as said below
- w_qkv: float32 [1024, 3072], P(('dp', 'fsdp')), may hold values from -0.25 to 0.25
- w_out: float32 [1024, 1024], P(('dp', 'fsdp')), may hold values from -0.5 to 0.5
- w_up: float32 [1024, 4096], P(('dp', 'fsdp')), may hold values from -0.1875 to 0.1875
- w_down: float32 [1024, 4096], P(('dp', 'fsdp')), may hold values from -0.09375 to 0.09375
- vectors: float32 [12, 1024], P(None, ('dp', 'fsdp')), as said below
- state_qkv: float32 [2, 1024, 3072], P(None, ('dp', 'fsdp')), as said below
- state_out: float32 [2, 1024, 1024], P(None, ('dp', 'fsdp')), as said below
- state_up: float32 [2, 1024, 4096], P(None, ('dp', 'fsdp')), as said below
- state_down: float32 [2, 1024, 4096], P(None, ('dp', 'fsdp')), as said below
- state_vectors: float32 [2, 12, 1024], P(None, None, ('dp', 'fsdp')), as said below
Outputs:
- activations: bfloat16 [4096, 1024], P(('dp', 'fsdp'))
- input_grad: float32 [4096, 1024], P(('dp', 'fsdp'))
- grad_w_qkv: float32 [1024, 3072], P(('dp', 'fsdp'))
- grad_w_out: float32 [1024, 1024], P(('dp', 'fsdp'))
- grad_w_up: float32 [1024, 4096], P(('dp', 'fsdp'))
- grad_w_down: float32 [1024, 4096], P(('dp', 'fsdp'))
- grad_vectors: float32 [12, 1024], P(None, ('dp', 'fsdp'))
- new_state_qkv: float32 [2, 1024, 3072], P(None, ('dp', 'fsdp'))
- new_state_out: float32 [2, 1024, 1024], P(None, ('dp', 'fsdp'))
- new_state_up: float32 [2, 1024, 4096], P(None, ('dp', 'fsdp'))
- new_state_down: float32 [2, 1024, 4096], P(None, ('dp', 'fsdp'))
- new_state_vectors: float32 [2, 12, 1024], P(None, None, ('dp', 'fsdp'))
- new_w_qkv: float32 [1024, 3072], P(('dp', 'fsdp'))
- new_w_out: float32 [1024, 1024], P(('dp', 'fsdp'))
- new_w_up: float32 [1024, 4096], P(('dp', 'fsdp'))
- new_w_down: float32 [1024, 4096], P(('dp', 'fsdp'))
- new_vectors: float32 [12, 1024], P(None, ('dp', 'fsdp'))
Inputs may be any that keep to these rules, and one draw needn't show every extreme that they name: `tile_len`: a tile whose tile_join is 1 has at least one valid row, and the tile before it has 32. `tile_join`: the first tile of each block of 2 tiles has 0. `vectors`: rows 0 and 5 are gains near 1, the others biases. `state_qkv`: index 0 holds first moments, index 1 second moments, which are positive. `state_out`: as state_qkv. `state_up`: as state_qkv. `state_down`: as state_qkv. `state_vectors`: as state_qkv.
All inputs are finite; a program needn't handle non-finite values.
Results may differ from a plain program's by a relative error of at most 0.012.
The roundings to bfloat16 on the way count: a program that leaves them out, or rounds other values in their place, can miss the bound.
Values may be sent and summed in bfloat16 or wider, within the bound.
A program may use at most 256 MiB of HBM per device.

v0:
```python
import jax
import jax.numpy as jnp
from jax import lax
from jax.sharding import PartitionSpec as P

D = 1024
HD = 64
FF = 4096
TILE = 32
TPM = 2
MB = 2
STEP = 10


rate_matrix = 0.06
rate_vector = 1.0
decay_matrix = 0.1


def layer_norm(values, gain_row, shift_row):
    centre = values - jnp.mean(values, axis=-1, keepdims=True)
    spread = jnp.mean(centre * centre, axis=-1, keepdims=True)
    return centre * lax.rsqrt(spread + 1e-05) * gain_row + shift_row


def gelu_tanh(values):
    return jax.nn.gelu(values, approximate=True)


def tile_masks(lengths, join_flags):
    sequence_ids = jnp.cumsum(1 - join_flags)
    places = jnp.arange(TILE, dtype=jnp.int32)
    valid_rows = (places[None, :] < lengths[:, None]).reshape(-1)
    owner_ids = jnp.broadcast_to(sequence_ids[:, None], (lengths.shape[0], TILE)).reshape(-1)
    return (valid_rows, owner_ids)


def allowed_pairs(valid_rows, owner_ids):
    places = jnp.arange(valid_rows.shape[0], dtype=jnp.int32)
    causal = places[:, None] >= places[None, :]
    same_seq = owner_ids[:, None] == owner_ids[None, :]
    both_valid = valid_rows[:, None] & valid_rows[None, :]
    return causal & same_seq & both_valid | (places[:, None] == places[None, :])


def block_allowed(lengths, join_flags):
    valid_rows, owner_ids = tile_masks(lengths, join_flags)
    return allowed_pairs(valid_rows, owner_ids)


def column_sum(values):
    return jnp.sum(values.astype(jnp.float32), axis=0)


def split_heads(values):
    return values.reshape(values.shape[0], -1, HD)


def masked_scores(query_rows, key_rows, allowed):
    scores = jnp.einsum(
        "qhd,khd->hqk",
        split_heads(query_rows),
        split_heads(key_rows),
        preferred_element_type=jnp.float32,
    ) * HD ** (-0.5)
    return jnp.where(allowed[None], scores, -1000000000.0)


def attend_forward(query_rows, key_rows, value_rows, allowed):
    scores = masked_scores(query_rows, key_rows, allowed)
    row_top = jnp.max(scores, axis=-1, keepdims=True)
    exp_scores = jnp.exp(scores - row_top)
    row_total = jnp.sum(exp_scores, axis=-1, keepdims=True)
    attn_weights = (exp_scores / row_total).astype(jnp.bfloat16)
    attended = jnp.einsum(
        "hqk,khd->qhd", attn_weights, split_heads(value_rows), preferred_element_type=jnp.float32
    )
    return (attended.reshape(query_rows.shape[0], -1), row_top + jnp.log(row_total))


def attend_backward(query_rows, key_rows, value_rows, allowed, log_total, grad_attended):
    score_scale = HD ** (-0.5)
    probabilities = jnp.exp(masked_scores(query_rows, key_rows, allowed) - log_total)
    grad_heads = split_heads(grad_attended)
    grad_values = jnp.einsum(
        "hqk,qhd->khd",
        probabilities.astype(jnp.bfloat16),
        grad_heads,
        preferred_element_type=jnp.float32,
    )
    grad_probs = jnp.einsum(
        "qhd,khd->hqk", grad_heads, split_heads(value_rows), preferred_element_type=jnp.float32
    )
    inner_sum = jnp.sum(grad_probs * probabilities, axis=-1, keepdims=True)
    grad_scores = (probabilities * (grad_probs - inner_sum)).astype(jnp.bfloat16)
    grad_queries = (
        jnp.einsum(
            "hqk,khd->qhd", grad_scores, split_heads(key_rows), preferred_element_type=jnp.float32
        )
        * score_scale
    )
    grad_keys = (
        jnp.einsum(
            "hqk,qhd->khd", grad_scores, split_heads(query_rows), preferred_element_type=jnp.float32
        )
        * score_scale
    )
    row_count = query_rows.shape[0]
    return jnp.concatenate(
        [
            grad_queries.reshape(row_count, -1),
            grad_keys.reshape(row_count, -1),
            grad_values.reshape(row_count, -1),
        ],
        axis=1,
    )


def fetch(pieces, vector_piece):
    gathered = (
        lax.all_gather(pieces[0], ("dp", "fsdp"), axis=0, tiled=True),
        lax.all_gather(pieces[1], ("dp", "fsdp"), axis=0, tiled=True),
        lax.all_gather(pieces[2], ("dp", "fsdp"), axis=0, tiled=True),
        lax.all_gather(pieces[3], ("dp", "fsdp"), axis=0, tiled=True),
        lax.all_gather(vector_piece, ("dp", "fsdp"), axis=1, tiled=True),
    )
    return gathered


def adamw(master, gradient, moments, step_rate, decay_rate):
    first_moment = 0.9 * moments[0] + 0.1 * gradient
    second_moment = 0.999 * moments[1] + 0.001 * gradient * gradient
    first_hat = first_moment / (1.0 - 0.9**STEP)
    second_hat = second_moment / (1.0 - 0.999**STEP)
    updated = master - step_rate * (
        first_hat / (jnp.sqrt(second_hat) + 1e-08) + decay_rate * master
    )
    return (jnp.stack([first_moment, second_moment]), updated)


def per_device(
    tokens,
    cotangent,
    tile_len,
    tile_join,
    w_qkv,
    w_out,
    w_up,
    w_down,
    vectors,
    state_qkv,
    state_out,
    state_up,
    state_down,
    state_vectors,
):
    masters = (w_qkv, w_out, w_up, w_down, vectors)
    rows_own = w_qkv.shape[0]
    pieces = (
        w_qkv.astype(jnp.bfloat16).reshape(rows_own, 3, -1),
        w_out.astype(jnp.bfloat16).reshape(rows_own, 1, -1),
        w_up.astype(jnp.bfloat16).reshape(rows_own, 1, -1),
        w_down.astype(jnp.bfloat16).reshape(rows_own, 1, -1),
    )
    vector_piece = vectors.astype(jnp.bfloat16)
    block_rows = TPM * TILE
    groups = 1
    group_lens, group_joins = (tile_len, tile_join)
    group_lens = group_lens.reshape(groups, MB, TPM)
    group_joins = group_joins.reshape(groups, MB, TPM)
    held_weights = fetch(pieces, vector_piece)
    saved = []
    results = []
    input_grads = []
    vector_grads = jnp.zeros((12, D), jnp.float32)
    for micro_batch in range(MB):
        row_start = micro_batch * block_rows
        inputs = tokens[row_start : row_start + block_rows].astype(jnp.float32)
        own_valid, own_owner = tile_masks(
            tile_len[micro_batch * TPM : (micro_batch + 1) * TPM],
            tile_join[micro_batch * TPM : (micro_batch + 1) * TPM],
        )
        allowed = jax.vmap(block_allowed)(group_lens[:, micro_batch], group_joins[:, micro_batch])
        full_weights = held_weights
        weight_qkv, weight_out, weight_up, weight_down, vector_rows = full_weights
        vector_rows = vector_rows.astype(jnp.float32)
        width_q = weight_qkv.shape[2]
        normed_one, pull_first = jax.vjp(layer_norm, inputs, vector_rows[0], vector_rows[1])
        first_in = normed_one.astype(jnp.bfloat16)
        bias_query = vector_rows[2]
        bias_value = vector_rows[3]
        bias_qkv = jnp.stack([bias_query, jnp.zeros_like(bias_query), bias_value])
        qkv = (
            jnp.einsum("rd,dkc->rkc", first_in, weight_qkv, preferred_element_type=jnp.float32)
            + bias_qkv
        ).astype(jnp.bfloat16)
        query_rows = qkv[:, 0].reshape(groups, block_rows, width_q)
        key_rows = qkv[:, 1].reshape(groups, block_rows, width_q)
        value_rows = qkv[:, 2].reshape(groups, block_rows, width_q)
        attended, log_total = jax.vmap(attend_forward)(query_rows, key_rows, value_rows, allowed)
        attended = attended.reshape(-1, width_q).astype(jnp.bfloat16)
        out_terms = jnp.einsum(
            "rc,nc->rn", attended, weight_out[:, 0], preferred_element_type=jnp.float32
        )
        middle = inputs + out_terms + vector_rows[4]
        normed_two, pull_second = jax.vjp(layer_norm, middle, vector_rows[5], vector_rows[6])
        second_in = normed_two.astype(jnp.bfloat16)
        bias_up = vector_rows[8:12].reshape(-1)
        hidden = jnp.dot(second_in, weight_up[:, 0], preferred_element_type=jnp.float32) + bias_up
        active, pull_gelu = jax.vjp(gelu_tanh, hidden)
        active = active.astype(jnp.bfloat16)
        down_terms = jnp.einsum(
            "rf,nf->rn", active, weight_down[:, 0], preferred_element_type=jnp.float32
        )
        result = middle + down_terms + vector_rows[7]
        results.append(result.astype(jnp.bfloat16))
        full_weights = held_weights
        weight_qkv, weight_out, weight_up, weight_down, vector_rows = full_weights
        grad_result = cotangent[row_start : row_start + block_rows].astype(jnp.float32) * own_valid[
            :, None
        ].astype(jnp.float32)
        grad_branch = grad_result.astype(jnp.bfloat16)
        grad_active = jnp.dot(grad_branch, weight_down[:, 0], preferred_element_type=jnp.float32)
        grad_hidden = pull_gelu(grad_active)[0].astype(jnp.bfloat16)
        second_terms = jnp.einsum(
            "rf,df->rd", grad_hidden, weight_up[:, 0], preferred_element_type=jnp.float32
        )
        grad_middle_norm, grad_gain_two, grad_shift_two = pull_second(second_terms)
        grad_middle = grad_result + grad_middle_norm
        grad_attn = grad_middle.astype(jnp.bfloat16)
        grad_attended = jnp.dot(
            grad_attn, weight_out[:, 0], preferred_element_type=jnp.float32
        ).astype(jnp.bfloat16)
        grad_qkv = jax.vmap(attend_backward)(
            query_rows,
            key_rows,
            value_rows,
            allowed,
            log_total,
            grad_attended.reshape(groups, block_rows, width_q),
        )
        grad_qkv = grad_qkv.reshape(-1, 3, width_q).astype(jnp.bfloat16)
        first_terms = jnp.einsum(
            "rkc,dkc->rd", grad_qkv, weight_qkv, preferred_element_type=jnp.float32
        )
        grad_input_norm, grad_gain_one, grad_shift_one = pull_first(first_terms)
        input_grads.append(grad_middle + grad_input_norm)
        small_rows = jnp.stack(
            [
                grad_gain_one,
                grad_shift_one,
                column_sum(grad_qkv[:, 0]),
                column_sum(grad_qkv[:, 2]),
                column_sum(grad_attn),
                grad_gain_two,
                grad_shift_two,
                column_sum(grad_branch),
            ]
        )
        hidden_rows = column_sum(grad_hidden).reshape(4, D)
        vector_grads = vector_grads + jnp.concatenate([small_rows, hidden_rows], axis=0)
        saved.append(
            (first_in, grad_qkv, grad_attn, attended, second_in, grad_hidden, grad_branch, active)
        )
    stacked = [jnp.concatenate([entry[place] for entry in saved], axis=0) for place in range(8)]
    vector_total = lax.psum_scatter(vector_grads, ("dp", "fsdp"), scatter_dimension=1, tiled=True)
    flat_qkv = stacked[1].reshape(stacked[1].shape[0], -1)
    terms = [
        jnp.einsum("rd,rc->dc", stacked[0], flat_qkv, preferred_element_type=jnp.float32),
        jnp.einsum("rn,rc->nc", stacked[2], stacked[3], preferred_element_type=jnp.float32),
        jnp.einsum("rd,rf->df", stacked[4], stacked[5], preferred_element_type=jnp.float32),
        jnp.einsum("rn,rf->nf", stacked[6], stacked[7], preferred_element_type=jnp.float32),
    ]
    joined = lax.psum_scatter(
        jnp.concatenate(terms, axis=1), ("dp", "fsdp"), scatter_dimension=0, tiled=True
    )
    reduced = (
        joined[:, : 3 * D],
        joined[:, 3 * D : 4 * D],
        joined[:, 4 * D : 4 * D + FF],
        joined[:, 4 * D + FF :],
        vector_total,
    )
    reduced = tuple((reduced[place] for place in range(5)))
    states = (state_qkv, state_out, state_up, state_down, state_vectors)
    step_rates = (rate_matrix, rate_matrix, rate_matrix, rate_matrix, rate_vector)
    decay_rates = (decay_matrix, decay_matrix, decay_matrix, decay_matrix, 0.0)
    updates = [
        adamw(masters[place], reduced[place], states[place], step_rates[place], decay_rates[place])
        for place in range(5)
    ]
    return (
        jnp.concatenate(results, axis=0),
        jnp.concatenate(input_grads, axis=0),
        reduced[0],
        reduced[1],
        reduced[2],
        reduced[3],
        reduced[4],
        updates[0][0],
        updates[1][0],
        updates[2][0],
        updates[3][0],
        updates[4][0],
        updates[0][1],
        updates[1][1],
        updates[2][1],
        updates[3][1],
        updates[4][1],
    )


def solution(mesh):
    return jax.shard_map(
        per_device,
        mesh=mesh,
        in_specs=(
            P(("dp", "fsdp"), None),
            P(("dp", "fsdp"), None),
            P(("dp", "fsdp")),
            P(("dp", "fsdp")),
            P(("dp", "fsdp"), None),
            P(("dp", "fsdp"), None),
            P(("dp", "fsdp"), None),
            P(("dp", "fsdp"), None),
            P(None, ("dp", "fsdp")),
            P(None, ("dp", "fsdp"), None),
            P(None, ("dp", "fsdp"), None),
            P(None, ("dp", "fsdp"), None),
            P(None, ("dp", "fsdp"), None),
            P(None, None, ("dp", "fsdp")),
        ),
        out_specs=(
            P(("dp", "fsdp"), None),
            P(("dp", "fsdp"), None),
            P(("dp", "fsdp"), None),
            P(("dp", "fsdp"), None),
            P(("dp", "fsdp"), None),
            P(("dp", "fsdp"), None),
            P(None, ("dp", "fsdp")),
            P(None, ("dp", "fsdp"), None),
            P(None, ("dp", "fsdp"), None),
            P(None, ("dp", "fsdp"), None),
            P(None, ("dp", "fsdp"), None),
            P(None, None, ("dp", "fsdp")),
            P(("dp", "fsdp"), None),
            P(("dp", "fsdp"), None),
            P(("dp", "fsdp"), None),
            P(("dp", "fsdp"), None),
            P(None, ("dp", "fsdp")),
        ),
        check_vma=False,
    )
```

profile of v0, /device:TPU:0, one launch (start us, length us, event | category | flops | bytes accessed | tf_op | source)
XLA Modules:
  0.0 961.7 jit_solution(5665733588845562678)
XLA Ops:
  18.7 44.0 %all-gather.3 = bf16[32,32,12]{1,2,0:T(8,128)(2,1)S(1)} all-gather(bf16[1,32,12]{1,2,0:T(8,128)(2,1)S(1)} %convert_bitcast_fusion), channel_id=1, replica_groups=mesh['dp'=8,'fsdp'=4] {'dp','fsdp'}, dimensions={0}, use_global_device_ids=true | all-gather | bytes 25344 | tf_op jit(solution)/shard_map/all_gather | solution.py:125
  70.8 12.8 %all-gather.9.cloned.1.call-done = bf16[1024,3,1024]{2,0,1:T(8,128)(2,1)} async-done(((bf16[32,3,1024]{2,0,1:T(8,128)(2,1)}), bf16[1024,3,1024]{2,0,1:T(8,128)(2,1)}) %all-gather.9.cloned.1.call-update) | async-done | bytes 6291472 | tf_op jit(solution)/shard_map/all_gather | solution.py:121
  83.7 4.0 fusion
  88.3 4.1 fusion.1
  93.7 48.7 %all-gather.11.cloned.1.call-done = bf16[1024,1024]{1,0:T(8,128)(2,1)} async-done(((bf16[32,1024]{1,0:T(8,128)(2,1)}), bf16[1024,1024]{1,0:T(8,128)(2,1)}) %all-gather.11.cloned.1.call-update) | async-done | bytes 2097168 | tf_op jit(solution)/shard_map/all_gather | solution.py:122
  142.4 2.4 fusion.160
  146.6 2.5 fusion.159
  151.4 70.8 %all-gather.15.cloned.1.call-done = bf16[1024,4096]{1,0:T(8,128)(2,1)} async-done(((bf16[32,4096]{1,0:T(8,128)(2,1)}), bf16[1024,4096]{1,0:T(8,128)(2,1)}) %all-gather.15.cloned.1.call-update) | async-done | bytes 8388624 | tf_op jit(solution)/shard_map/all_gather | solution.py:124
  222.2 6.1 fusion.163
  229.9 71.6 %all-gather.13.cloned.1.call-done = bf16[1024,4096]{1,0:T(8,128)(2,1)} async-done(((bf16[32,4096]{1,0:T(8,128)(2,1)}), bf16[1024,4096]{1,0:T(8,128)(2,1)}) %all-gather.13.cloned.1.call-update) | async-done | bytes 8388624 | tf_op jit(solution)/shard_map/all_gather | solution.py:123
  301.6 7.2 convert_reduce_fusion
  309.5 2.8 fusion.165
  312.4 3.7 convert_reduce_fusion.1
  316.2 3.4 multiply_reduce_fusion.3
  325.0 1.9 fusion.71
  329.1 2.0 fusion.2
  331.0 2.0 fusion.3
  333.0 2.0 convolution_convert_fusion.3
  346.3 4.0 fusion.82
  350.4 9.3 fusion.28
  362.1 4.9 convolution_bitcast_fusion
  367.0 4.9 fusion.68
  374.5 6.3 fusion.36
  380.9 8.2 fusion.32
  389.1 34.0 %pad_maximum_fusion = f32[1024,12288]{1,0:T(8,128)} fusion(f32[1024,4096]{1,0:T(8,128)} %fusion.32, f32[1024,4096]{1,0:T(8,128)} %fusion.28, f32[1024,1024]{1,0:T(8,128)} %fusion.82, f32[1024,3072]{1,0:T(8,128)} %fusion.36), kind=kLoop, calls=%fused_computation | loop fusion | flops 37748736 | bytes 100663296 | tf_op jit(solution)/shard_map/concatenate | solution.py:275
  424.7 6.2 fusion.12
  430.9 6.2 fusion.13
  439.3 67.6 %reduce-scatter.7.cloned.1.call-done = f32[32,12]{1,0:T(8,128)} async-done(((f32[1024,12]{1,0:T(8,128)}), f32[32,12]{1,0:T(8,128)}) %reduce-scatter.7.cloned.1.call-update) | async-done | bytes 1552
  509.6 432.2 %reduce-scatter.5.cloned.1.call-done = f32[32,12288]{1,0:T(8,128)} async-done(((f32[1024,12288]{1,0:T(8,128)}), f32[32,12288]{1,0:T(8,128)}) %reduce-scatter.5.cloned.1.call-update) | async-done | bytes 1572880 | tf_op jit(solution)/shard_map/reduce_scatter | solution.py:274
  941.8 1.8 multiply_subtract_fusion.3
  944.7 2.2 multiply_subtract_fusion.2
  947.0 3.3 multiply_subtract_fusion
  (370 shorter events, 62.1 us)
Async XLA Ops:
  7.2 76.5 %all-gather.9.cloned.1.call-start = ((), (), s32[]{:S(2)}) async-start(), calls=%async_computation.2 | async-start | bytes 6488064 | tf_op jit(solution)/shard_map/all_gather | solution.py:121
  9.0 133.4 %all-gather.11.cloned.1.call-start = ((), (), s32[]{:S(2)}) async-start(), calls=%async_computation.4 | async-start | bytes 2162688 | tf_op jit(solution)/shard_map/all_gather | solution.py:122
  10.6 211.6 %all-gather.15.cloned.1.call-start = ((), (), s32[]{:S(2)}) async-start(), calls=%async_computation.6 | async-start | bytes 8650752 | tf_op jit(solution)/shard_map/all_gather | solution.py:124
  12.4 289.1 %all-gather.13.cloned.1.call-start = ((), (), s32[]{:S(2)}) async-start(), calls=%async_computation.5 | async-start | bytes 8650752 | tf_op jit(solution)/shard_map/all_gather | solution.py:123
  14.3 492.6 %reduce-scatter.7.cloned.1.call-start = ((), (), s32[]{:S(2)}) async-start(), calls=%async_computation.7 | async-start | bytes 540672
  64.7 19.0 %copy-start.60 = (f32[64]{0:T(128)}, f32[64]{0:T(128)S(1)}, u32[]{:S(2)}) copy-start(f32[64]{0:T(128)S(1)} %get-tuple-element.202) | copy-start | bytes 772
  64.7 27.7 %copy-start.57 = (f32[64]{0:T(128)}, f32[64]{0:T(128)S(1)}, u32[]{:S(2)}) copy-start(f32[64]{0:T(128)S(1)} %get-tuple-element.201) | copy-start | bytes 772
  69.5 158.8 %copy-start.34 = (bf16[64,1024]{1,0:T(8,128)(2,1)}, bf16[64,1024]{1,0:T(8,128)(2,1)S(1)}, u32[]{:S(2)}) copy-start(bf16[64,1024]{1,0:T(8,128)(2,1)S(1)} %get-tuple-element.156) | copy-start | bytes 393220
  70.8 21.8 %copy-start.42 = (bf16[64,1024]{1,0:T(8,128)(2,1)}, bf16[64,1024]{1,0:T(8,128)(2,1)S(1)}, u32[]{:S(2)}) copy-start(bf16[64,1024]{1,0:T(8,128)(2,1)S(1)} %get-tuple-element.152) | copy-start | bytes 393220
  87.7 54.7 %copy-start.2 = (bf16[128,1024]{1,0:T(8,128)(2,1)S(1)}, bf16[128,1024]{1,0:T(8,128)(2,1)}, u32[]{:S(2)}) copy-start(bf16[128,1024]{1,0:T(8,128)(2,1)} %param.14) | copy-start | bytes 786436
  87.9 58.3 %copy-start.46 = (bf16[64,16,64]{2,1,0:T(8,128)(2,1)}, bf16[64,16,64]{2,1,0:T(8,128)(2,1)S(1)}, u32[]{:S(2)}) copy-start(bf16[64,16,64]{2,1,0:T(8,128)(2,1)S(1)} %reshape.840) | copy-start | bytes 393220
  88.1 58.0 %copy-start.16 = (bf16[64,1,1024]{0,2,1:T(8,128)(2,1)}, bf16[64,1,1024]{0,2,1:T(8,128)(2,1)S(1)}, u32[]{:S(2)}) copy-start(bf16[64,1,1024]{0,2,1:T(8,128)(2,1)S(1)} %copy.207) | copy-start | bytes 393220
  88.3 57.8 %copy-start.18 = (bf16[64,1,1024]{0,2,1:T(8,128)(2,1)}, bf16[64,1,1024]{0,2,1:T(8,128)(2,1)S(1)}, u32[]{:S(2)}) copy-start(bf16[64,1,1024]{0,2,1:T(8,128)(2,1)S(1)} %copy.206) | copy-start | bytes 393220
  92.6 53.5 %copy-start.47 = (bf16[64,16,64]{2,1,0:T(8,128)(2,1)}, bf16[64,16,64]{2,1,0:T(8,128)(2,1)S(1)}, u32[]{:S(2)}) copy-start(bf16[64,16,64]{2,1,0:T(8,128)(2,1)S(1)} %reshape.849) | copy-start | bytes 393220
  92.8 135.4 %copy-start.19 = (bf16[64,1,1024]{0,2,1:T(8,128)(2,1)}, bf16[64,1,1024]{0,2,1:T(8,128)(2,1)S(1)}, u32[]{:S(2)}) copy-start(bf16[64,1,1024]{0,2,1:T(8,128)(2,1)S(1)} %copy.209) | copy-start | bytes 393220
  93.0 135.3 %copy-start.20 = (bf16[64,1,1024]{0,2,1:T(8,128)(2,1)}, bf16[64,1,1024]{0,2,1:T(8,128)(2,1)S(1)}, u32[]{:S(2)}) copy-start(bf16[64,1,1024]{0,2,1:T(8,128)(2,1)S(1)} %copy.208) | copy-start | bytes 393220
  93.7 134.5 %copy-start.44 = (bf16[16,64,64]{2,1,0:T(8,128)(2,1)}, bf16[16,64,64]{2,1,0:T(8,128)(2,1)S(1)}, u32[]{:S(2)}) copy-start(bf16[16,64,64]{2,1,0:T(8,128)(2,1)S(1)} %convolution_convert_fusion) | copy-start | bytes 393220
  144.9 83.4 %copy-start.80 = (f32[64]{0:T(128)}, f32[64]{0:T(128)S(1)}, u32[]{:S(2)}) copy-start(f32[64]{0:T(128)S(1)} %broadcast_multiply_fusion) | copy-start | bytes 772
  146.5 81.7 %copy-start.45 = (bf16[16,64,64]{2,1,0:T(8,128)(2,1)}, bf16[16,64,64]{2,1,0:T(8,128)(2,1)S(1)}, u32[]{:S(2)}) copy-start(bf16[16,64,64]{2,1,0:T(8,128)(2,1)S(1)} %convolution_convert_fusion.1) | copy-start | bytes 393220
  149.1 79.2 %copy-start.82 = (f32[64]{0:T(128)}, f32[64]{0:T(128)S(1)}, u32[]{:S(2)}) copy-start(f32[64]{0:T(128)S(1)} %broadcast_multiply_fusion.2) | copy-start | bytes 772
  149.3 79.0 %copy-start.90 = (f32[64]{0:T(128)}, f32[64]{0:T(128)S(1)}, u32[]{:S(2)}) copy-start(f32[64]{0:T(128)S(1)} %fusion.137) | copy-start | bytes 772
  149.9 78.4 %copy-start.92 = (f32[64]{0:T(128)}, f32[64]{0:T(128)S(1)}, u32[]{:S(2)}) copy-start(f32[64]{0:T(128)S(1)} %fusion.135) | copy-start | bytes 772
  151.4 150.2 %copy-start.51 = (bf16[64,1024]{1,0:T(8,128)(2,1)}, bf16[64,1024]{1,0:T(8,128)(2,1)S(1)}, u32[]{:S(2)}) copy-start(bf16[64,1024]{1,0:T(8,128)(2,1)S(1)} %get-tuple-element.171) | copy-start | bytes 393220
  151.4 161.1 %copy-start.50 = (bf16[64,1024]{1,0:T(8,128)(2,1)}, bf16[64,1024]{1,0:T(8,128)(2,1)S(1)}, u32[]{:S(2)}) copy-start(bf16[64,1024]{1,0:T(8,128)(2,1)S(1)} %get-tuple-element.170) | copy-start | bytes 393220
  228.3 73.2 %copy-start.70 = (f32[1,8,4,128]{3,1,2,0:T(8,128)S(1)}, f32[1,8,4,128]{3,1,2,0:T(8,128)}, u32[]{:S(2)}) copy-start(f32[1,8,4,128]{3,1,2,0:T(8,128)} %copy.254) | copy-start | bytes 49156
  374.2 567.6 %reduce-scatter.5.cloned.1.call-start = ((), (), s32[]{:S(2)}) async-start(), calls=%async_computation.3 | async-start | bytes 51904512 | tf_op jit(solution)/shard_map/reduce_scatter | solution.py:274
  430.8 76.8 %copy-start.56 = (f32[12,32]{1,0:T(8,128)S(1)}, f32[12,32]{1,0:T(8,128)}, u32[]{:S(2)}) copy-start(f32[12,32]{1,0:T(8,128)} %param.22) | copy-start | bytes 4612
  430.8 511.0 %copy-start.53 = (f32[32,1024]{1,0:T(8,128)S(1)}, f32[32,1024]{1,0:T(8,128)}, u32[]{:S(2)}) copy-start(f32[32,1024]{1,0:T(8,128)} %param.19) | copy-start | bytes 393220
  430.9 513.8 %copy-start.11 = (f32[2,32,3072]{2,1,0:T(8,128)S(1)}, f32[2,32,3072]{2,1,0:T(8,128)}, u32[]{:S(2)}) copy-start(f32[2,32,3072]{2,1,0:T(8,128)} %param.23) | copy-start | bytes 2359300
  430.9 516.1 %copy-start.9 = (f32[2,32,4096]{2,1,0:T(8,128)S(1)}, f32[2,32,4096]{2,1,0:T(8,128)}, u32[]{:S(2)}) copy-start(f32[2,32,4096]{2,1,0:T(8,128)} %param.26) | copy-start | bytes 3145732
  430.9 516.1 %copy-start.10 = (f32[2,32,4096]{2,1,0:T(8,128)S(1)}, f32[2,32,4096]{2,1,0:T(8,128)}, u32[]{:S(2)}) copy-start(f32[2,32,4096]{2,1,0:T(8,128)} %param.25) | copy-start | bytes 3145732
  507.6 443.0 %copy-start.55 = (f32[12,32]{1,0:T(8,128)}, f32[12,32]{1,0:T(8,128)S(1)}, u32[]{:S(2)}) copy-start(f32[12,32]{1,0:T(8,128)S(1)} %copy.203) | copy-start | bytes 4612
  (88 other events, 784.6 us)
Sparse Core Ops, SparseCore 0:
  11.5 72.1 all-gather.8
  87.1 55.2 all-gather.10
  145.8 76.2 all-gather.14
  225.5 76.0 all-gather.12
  374.3 132.4 reduce-scatter.6
  514.3 427.5 reduce-scatter.4
where the time goes:
time: 972 us; the launch traced here: 962 us
  waiting for transfers between devices  704 us (72%)
  matrix products  104 us (11%)
  other arithmetic  71.3 us (7%)
  blocking collectives  44 us (5%)
  local copies, waits for them, and re-layouts  21.8 us (2%)
  between operations  16.3 us (2%)
    reduce_scatter x1, waiting for transfers between devices, per_device(): lax.psum_scatter(jnp.concatenate(terms, axis=1), ('dp', 'fsdp'), scatter_...  432 us
    all_gather x1, waiting for transfers between devices, fetch(): lax.all_gather(pieces[2], ('dp', 'fsdp'), axis=0, tiled=True)  71.6 us
    all_gather x1, waiting for transfers between devices, fetch(): lax.all_gather(pieces[3], ('dp', 'fsdp'), axis=0, tiled=True)  70.8 us
    unnamed x7, waiting for transfers between devices  67.7 us
    all_gather x1, waiting for transfers between devices, fetch(): lax.all_gather(pieces[1], ('dp', 'fsdp'), axis=0, tiled=True)  48.7 us
    all_gather x1, blocking collectives, fetch(): lax.all_gather(vector_piece, ('dp', 'fsdp'), axis=1, tiled=True)  44 us
    concatenate x1, other arithmetic, per_device(): jnp.concatenate(terms, axis=1)  34 us
  transfers between devices with their start and end apart: 6, of which 6 were waited for; matrix products, arithmetic and copies ran while one was open for 11% of the time, Pallas kernels for 0%

commit v1 on v0

v1 whole, which is shorter than its diff:
```python
import functools

import jax
import jax.numpy as jnp
from jax import lax
from jax.experimental import pallas as pl
from jax.experimental.pallas import tpu as pltpu
from jax.sharding import PartitionSpec as P

D = 1024
HD = 64
FF = 4096
TILE = 32
TPM = 2
STEP = 10
BLOCK = TPM * TILE
EPS = 1e-05
VEC_PAD = 128
SCALE = HD**-0.5

rate_matrix = 0.06
rate_vector = 1.0
decay_matrix = 0.1

BF = jnp.bfloat16
F32 = jnp.float32
NN = (((1,), (0,)), ((), ()))
NT = (((1,), (1,)), ((), ()))
TN = (((0,), (0,)), ((), ()))


def dot(left, right, dims=NN):
    return lax.dot_general(left, right, dims, preferred_element_type=F32)


def normalize(values):
    centre = values - jnp.mean(values, axis=-1, keepdims=True)
    spread = jnp.mean(centre * centre, axis=-1, keepdims=True)
    inverse = lax.rsqrt(spread + EPS)
    return centre * inverse, inverse


def norm_backward(grads, gain, normed, inverse):
    scaled = grads * gain
    return inverse * (
        scaled
        - jnp.mean(scaled, axis=-1, keepdims=True)
        - normed * jnp.mean(scaled * normed, axis=-1, keepdims=True)
    )


def gelu_and_slope(values):
    root = (2.0 / jnp.pi) ** 0.5
    square = values * values
    bent = jnp.tanh(root * values * (1.0 + 0.044715 * square))
    half = 0.5 * (1.0 + bent)
    slope = half + 0.5 * values * (1.0 - bent * bent) * root * (1.0 + 3 * 0.044715 * square)
    return values * half, slope


def probabilities(query, key, mask):
    scores = jnp.where(mask, dot(query, key, NT) * SCALE, -1000000000.0)
    exp_scores = jnp.exp(scores - jnp.max(scores, axis=-1, keepdims=True))
    return exp_scores / jnp.sum(exp_scores, axis=-1, keepdims=True)


def attend_kernel(width, qkv_ref, mask_ref, out_ref):
    mask = mask_ref[...] > 0.5
    heads = []
    for at in range(0, width, HD):
        query = qkv_ref[:, at : at + HD]
        key = qkv_ref[:, width + at : width + at + HD]
        value = qkv_ref[:, 2 * width + at : 2 * width + at + HD]
        probs = probabilities(query, key, mask).astype(BF)
        heads.append(dot(probs, value))
    out_ref[...] = jnp.concatenate(heads, axis=1).astype(BF)


def attend_back_kernel(width, qkv_ref, mask_ref, grad_ref, out_ref):
    mask = mask_ref[...] > 0.5
    grad_q, grad_k, grad_v = [], [], []
    for at in range(0, width, HD):
        query = qkv_ref[:, at : at + HD]
        key = qkv_ref[:, width + at : width + at + HD]
        value = qkv_ref[:, 2 * width + at : 2 * width + at + HD]
        grad = grad_ref[:, at : at + HD]
        probs = probabilities(query, key, mask)
        grad_probs = dot(grad, value, NT)
        inner = jnp.sum(grad_probs * probs, axis=-1, keepdims=True)
        grad_scores = (probs * (grad_probs - inner)).astype(BF)
        grad_q.append(dot(grad_scores, key) * SCALE)
        grad_k.append(dot(grad_scores, query, TN) * SCALE)
        grad_v.append(dot(probs.astype(BF), grad, TN))
    out_ref[...] = jnp.concatenate(grad_q + grad_k + grad_v, axis=1).astype(BF)


def attention_call(kernel, own, width, out_width, name, *operands):
    total = operands[0].shape[0]
    return pl.pallas_call(
        functools.partial(kernel, width),
        grid=(total // own,),
        in_specs=[pl.BlockSpec((own, item.shape[1]), lambda i: (i, 0)) for item in operands],
        out_specs=pl.BlockSpec((own, out_width), lambda i: (i, 0)),
        out_shape=jax.ShapeDtypeStruct((total, out_width), BF),
        compiler_params=pltpu.CompilerParams(vmem_limit_bytes=32 * 1024 * 1024),
        name=name,
    )(*operands)


def row_codes(lengths, joins):
    per_block = joins.reshape(-1, TPM)
    sequence = jnp.cumsum(1 - per_block, axis=1)
    block = jnp.arange(per_block.shape[0], dtype=jnp.int32)[:, None]
    owner = (block * (TPM + 1) + sequence).reshape(-1)
    places = jnp.arange(TILE, dtype=jnp.int32)
    valid = (places[None, :] < lengths[:, None]).reshape(-1)
    codes = jnp.repeat(owner, TILE)
    rows = jnp.arange(codes.shape[0], dtype=jnp.int32)
    return valid, jnp.where(valid, codes, -1 - rows)


def gather_rows(values, ways):
    pieces = [values]
    for step in range(1, ways):
        order = [(place, (place + step) % ways) for place in range(ways)]
        pieces.append(lax.ppermute(values, "fsdp", order))
    return jnp.concatenate(pieces, axis=0)


def sum_rows(partial, ways):
    own = partial.shape[0] // ways
    total = partial[:own]
    for step in range(1, ways):
        order = [(place, (place - step) % ways) for place in range(ways)]
        piece = partial[step * own : (step + 1) * own].astype(BF)
        total = total + lax.ppermute(piece, "fsdp", order).astype(F32)
    return total


def exchange(values):
    return lax.all_to_all(values, "fsdp", split_axis=0, concat_axis=0, tiled=True)


def adamw(master, gradient, moments, step_rate, decay_rate):
    first_moment = 0.9 * moments[0] + 0.1 * gradient
    second_moment = 0.999 * moments[1] + 0.001 * gradient * gradient
    first_hat = first_moment / (1.0 - 0.9**STEP)
    second_hat = second_moment / (1.0 - 0.999**STEP)
    updated = master - step_rate * (
        first_hat / (jnp.sqrt(second_hat) + 1e-08) + decay_rate * master
    )
    return (jnp.stack([first_moment, second_moment]), updated)


def column_parts(weight, ways):
    rows = weight.shape[0]
    return weight.astype(BF).reshape(rows, ways, -1).transpose(1, 0, 2)


def column_whole(parts):
    return parts.transpose(1, 0, 2).reshape(parts.shape[1], -1)


def per_device(
    ways,
    tokens,
    cotangent,
    tile_len,
    tile_join,
    w_qkv,
    w_out,
    w_up,
    w_down,
    vectors,
    state_qkv,
    state_out,
    state_up,
    state_down,
    state_vectors,
):
    masters = (w_qkv, w_out, w_up, w_down, vectors)
    rows_own = w_qkv.shape[0]
    own = tokens.shape[0]
    width = D // ways
    hidden_width = FF // ways
    me = lax.axis_index("fsdp")

    with jax.named_scope("weights"):
        qkv_parts = (
            w_qkv.astype(BF).reshape(rows_own, 3, ways, width).transpose(2, 0, 1, 3)
        ).reshape(ways, rows_own, 3 * width)
        vector_part = jnp.pad(vectors.T, ((0, 0), (0, VEC_PAD - vectors.shape[0]))).astype(BF)
        first_payload = jnp.concatenate(
            [
                qkv_parts,
                column_parts(w_out, ways),
                jnp.broadcast_to(vector_part[None], (ways, rows_own, VEC_PAD)),
            ],
            axis=2,
        )
        second_payload = jnp.concatenate(
            [column_parts(w_up, ways), column_parts(w_down, ways)], axis=2
        )
        first_rows = exchange(first_payload).reshape(ways * rows_own, -1)
        first_weights = lax.all_gather(first_rows, "dp", axis=0, tiled=True)
        second_rows = exchange(second_payload).reshape(ways * rows_own, -1)
        second_weights = lax.all_gather(second_rows, "dp", axis=0, tiled=True)

    with jax.named_scope("rows"):
        valid, codes = row_codes(tile_len, tile_join)
        grad_branch = jnp.where(valid[:, None], cotangent, jnp.zeros_like(cotangent))
        all_tokens = gather_rows(tokens, ways)
        all_branch = gather_rows(grad_branch, ways)
        all_codes = gather_rows(codes, ways).reshape(ways, own)
        places = jnp.arange(own, dtype=jnp.int32)
        causal = places[:, None] >= places[None, :]
        mask = (all_codes[:, :, None] == all_codes[:, None, :]) & causal[None]
        mask = mask.astype(F32).reshape(ways * own, own)

    weight_qkv = first_weights[:, : 3 * width]
    weight_out = first_weights[:, 3 * width : 4 * width]
    vector_rows = first_weights[:, 4 * width : 4 * width + vectors.shape[0]].T.astype(F32)
    bias_query = lax.dynamic_slice(vector_rows[2], (me * width,), (width,))
    bias_value = lax.dynamic_slice(vector_rows[3], (me * width,), (width,))
    bias_qkv = jnp.concatenate([bias_query, jnp.zeros_like(bias_query), bias_value])
    bias_up = lax.dynamic_slice(
        vector_rows[8:12].reshape(-1), (me * hidden_width,), (hidden_width,)
    )

    with jax.named_scope("forward"):
        inputs = tokens.astype(F32)
        all_normed, _ = normalize(all_tokens.astype(F32))
        first_in = (all_normed * vector_rows[0] + vector_rows[1]).astype(BF)
        qkv = (dot(first_in, weight_qkv) + bias_qkv).astype(BF)
        attended = attention_call(attend_kernel, own, width, width, "attend", qkv, mask)
        out_terms = sum_rows(dot(attended, weight_out, NT), ways)
        middle = inputs + out_terms + vector_rows[4]
        normed_two, inverse_two = normalize(middle)
        second_own = (normed_two * vector_rows[5] + vector_rows[6]).astype(BF)
        second_in = gather_rows(second_own, ways)

    weight_up = second_weights[:, :hidden_width]
    weight_down = second_weights[:, hidden_width:]

    with jax.named_scope("branch"):
        hidden = dot(second_in, weight_up) + bias_up
        active, slope = gelu_and_slope(hidden)
        active = active.astype(BF)
        grad_hidden = (dot(all_branch, weight_down) * slope).astype(BF)
        second_terms = sum_rows(dot(grad_hidden, weight_up, NT), ways)

    with jax.named_scope("branch_sums"):
        branch_grads = jnp.concatenate(
            [dot(second_in, grad_hidden, TN), dot(all_branch, active, TN)], axis=1
        )
        branch_total = lax.psum_scatter(branch_grads, "dp", scatter_dimension=0, tiled=True)

    with jax.named_scope("backward"):
        grad_result = grad_branch.astype(F32)
        grad_middle = grad_result + norm_backward(
            second_terms, vector_rows[5], normed_two, inverse_two
        )
        grad_attn = grad_middle.astype(BF)
        all_attn = gather_rows(grad_attn, ways)
        grad_attended = dot(all_attn, weight_out).astype(BF)
        grad_qkv = attention_call(
            attend_back_kernel, own, width, 3 * width, "attend_back", qkv, mask, grad_attended
        )
        first_terms = sum_rows(dot(grad_qkv, weight_qkv, NT), ways)
        normed_one, inverse_one = normalize(inputs)
        input_grad = grad_middle + norm_backward(
            first_terms, vector_rows[0], normed_one, inverse_one
        )

    with jax.named_scope("result"):
        down_terms = sum_rows(dot(active, weight_down, NT), ways)
        result = (middle + down_terms + vector_rows[7]).astype(BF)

    with jax.named_scope("attention_sums"):
        qkv_sums = jnp.sum(grad_qkv.astype(F32), axis=0)
        hidden_sums = jnp.sum(grad_hidden.astype(F32), axis=0)
        blank = jnp.zeros((D,), F32)
        vector_sums = jnp.stack(
            [
                jnp.sum(first_terms * normed_one, axis=0),
                jnp.sum(first_terms, axis=0),
                lax.dynamic_update_slice(blank, qkv_sums[:width], (me * width,)),
                lax.dynamic_update_slice(blank, qkv_sums[2 * width :], (me * width,)),
                jnp.sum(grad_attn.astype(F32), axis=0),
                jnp.sum(second_terms * normed_two, axis=0),
                jnp.sum(second_terms, axis=0),
                jnp.sum(grad_result, axis=0),
            ]
        )
        hidden_rows = lax.dynamic_update_slice(
            jnp.zeros((FF,), F32), hidden_sums, (me * hidden_width,)
        ).reshape(4, D)
        vector_sums = jnp.concatenate([vector_sums, hidden_rows], axis=0)
        attention_grads = jnp.concatenate(
            [
                dot(first_in, grad_qkv, TN),
                dot(all_attn, attended, TN),
                jnp.pad(vector_sums.T, ((0, 0), (0, VEC_PAD - vectors.shape[0]))),
            ],
            axis=1,
        )
        attention_total = lax.psum_scatter(attention_grads, "dp", scatter_dimension=0, tiled=True)

    with jax.named_scope("owners"):
        branch_parts = exchange(branch_total.reshape(ways, rows_own, -1))
        attention_parts = exchange(attention_total.reshape(ways, rows_own, -1))
        qkv_total = (
            attention_parts[:, :, : 3 * width]
            .reshape(ways, rows_own, 3, width)
            .transpose(1, 2, 0, 3)
            .reshape(rows_own, 3 * D)
        )
        reduced = (
            qkv_total,
            column_whole(attention_parts[:, :, 3 * width : 4 * width]),
            column_whole(branch_parts[:, :, :hidden_width]),
            column_whole(branch_parts[:, :, hidden_width:]),
            jnp.sum(attention_parts[:, :, 4 * width : 4 * width + vectors.shape[0]], axis=0).T,
        )
    states = (state_qkv, state_out, state_up, state_down, state_vectors)
    step_rates = (rate_matrix, rate_matrix, rate_matrix, rate_matrix, rate_vector)
    decay_rates = (decay_matrix, decay_matrix, decay_matrix, decay_matrix, 0.0)
    with jax.named_scope("adamw"):
        updates = [
            adamw(
                masters[place], reduced[place], states[place], step_rates[place], decay_rates[place]
            )
            for place in range(5)
        ]
    return (
        result,
        input_grad,
        *reduced,
        *(update[0] for update in updates),
        *(update[1] for update in updates),
    )


def solution(mesh):
    rows = P(("dp", "fsdp"), None)
    flat = P(("dp", "fsdp"))
    cols = P(None, ("dp", "fsdp"))
    moments = P(None, ("dp", "fsdp"), None)
    vector_moments = P(None, None, ("dp", "fsdp"))
    return jax.shard_map(
        functools.partial(per_device, mesh.shape["fsdp"]),
        mesh=mesh,
        in_specs=(
            rows, rows, flat, flat, rows, rows, rows, rows, cols,
            moments, moments, moments, moments, vector_moments,
        ),
        out_specs=(
            rows, rows, rows, rows, rows, rows, cols,
            moments, moments, moments, moments, vector_moments,
            rows, rows, rows, rows, cols,
        ),
        check_vma=False,
    )
```

time: 972 us -> 520 us (0.53)
  waiting for transfers between devices: 704 us -> 355 us
  matrix products: 104 us -> 26.8 us
  other arithmetic: 71.3 us -> 30.6 us
  starting transfers between devices: 0.5 us -> 32.4 us
  blocking collectives: 44 us -> 22.3 us
  Pallas kernels: 0 us -> 14.5 us
    reduce_scatter x1 -> x2, waiting for transfers between devices: 432 us -> 214 us  [the longest x1 131 us: per_device(): lax.psum_scatter(branch_grads, 'dp', scatter_dimension=0, tiled=True)]
    all_gather x4 -> x2, waiting for transfers between devices: 204 us -> 56.6 us  [the longest x1 32.1 us: per_device(): second_weights = lax.all_gather(second_rows, 'dp', axis=0, tiled=True)]
    dot_general x32 -> x12, matrix products: 104 us -> 26.8 us  [dot(): return lax.dot_general(left, right, dims, preferred_element_type=F32)]
    unnamed x7 -> x4, waiting for transfers between devices: 67.7 us -> 0.07 us
    ppermute x0 -> x27, waiting for transfers between devices: none -> 63.6 us  [the longest x12 34.8 us: sum_rows(): total = total + lax.ppermute(piece, 'fsdp', order).astype(F32)]
    all_gather x1 -> x0, blocking collectives: 44 us -> none  [fetch(): lax.all_gather(vector_piece, ('dp', 'fsdp'), axis=1, tiled=True)]
    concatenate x3 -> x7, other arithmetic: 35.6 us -> 9.22 us  [the longest x1 4.74 us: per_device(): jnp.concatenate([dot(first_in, grad_qkv, TN), dot(all_attn, attended, TN)...]
    ppermute x0 -> x27, starting transfers between devices: none -> 25 us  [the longest x15 15.3 us: gather_rows(): pieces.append(lax.ppermute(values, 'fsdp', order))]
  transfers between devices with their start and end apart: 6 -> 33, of which waited for: 6 -> 24; matrix products, arithmetic and copies ran while one was open for 11% -> 8% of each run, Pallas kernels for 0% -> 1%
where the time goes in v1:
time: 520 us; the launch traced here: 519 us
  waiting for transfers between devices  355 us (68%)
  starting transfers between devices  32.4 us (6%)
  other arithmetic  30.6 us (6%)
  matrix products  26.8 us (5%)
  local copies, waits for them, and re-layouts  22.8 us (4%)
  blocking collectives  22.3 us (4%)
  between operations  14.6 us (3%)
  Pallas kernels  14.5 us (3%)
    reduce_scatter x1, waiting for transfers between devices, per_device(): lax.psum_scatter(branch_grads, 'dp', scatter_dimension=0, tiled=True)  131 us
    reduce_scatter x1, waiting for transfers between devices, per_device(): lax.psum_scatter(attention_grads, 'dp', scatter_dimension=0, tiled=True)  82.9 us
    ppermute x12, waiting for transfers between devices, sum_rows(): total = total + lax.ppermute(piece, 'fsdp', order).astype(F32)  34.8 us
    all_gather x1, waiting for transfers between devices, per_device(): second_weights = lax.all_gather(second_rows, 'dp', axis=0, tiled=True)  32.1 us
    ppermute x15, waiting for transfers between devices, gather_rows(): pieces.append(lax.ppermute(values, 'fsdp', order))  28.9 us
    dot_general x12, matrix products, dot(): return lax.dot_general(left, right, dims, preferred_element_type=F32)  26.8 us
    all_gather x1, waiting for transfers between devices, per_device(): first_weights = lax.all_gather(first_rows, 'dp', axis=0, tiled=True)  24.5 us
    all_to_all x2, blocking collectives, exchange(): lax.all_to_all(values, 'fsdp', split_axis=0, concat_axis=0, tiled=True)  22.3 us
  transfers between devices with their start and end apart: 33, of which 24 were waited for; matrix products, arithmetic and copies ran while one was open for 8% of the time, Pallas kernels for 1%

profile of v1, /device:TPU:0, one launch (start us, length us, event | category | flops | bytes accessed | tf_op | source)
XLA Modules:
  0.0 518.6 jit_solution(10567730361014525215)
XLA Ops:
  10.6 10.4 %all_to_all.20 = bf16[4,32,1152]{2,1,0:T(8,128)(2,1)S(1)} all-to-all(bf16[4,32,1152]{2,1,0:T(8,128)(2,1)S(1)} %pad_maximum_fusion.9), channel_id=1, replica_groups=mesh['dp'=8,'fsdp'=4] {'fsdp'}, dimensions={0} | all-to-all | bytes 589824 | tf_op jit(solution)/shard_map/weights/all_to_all | solution.py:141
  23.1 11.9 %all_to_all.21 = bf16[4,32,2048]{2,1,0:T(8,128)(2,1)} all-to-all(bf16[4,32,2048]{2,1,0:T(8,128)(2,1)S(1)} %copy.113), channel_id=1, replica_groups=mesh['dp'=8,'fsdp'=4] {'fsdp'}, dimensions={0} | all-to-all | bytes 1048576 | tf_op jit(solution)/shard_map/weights/all_to_all | solution.py:141
  40.1 7.3 %collective-permute-done.5 = s32[128]{0:T(128)S(1)} collective-permute-done((s32[128]{0:T(128)S(1)}, s32[128]{0:T(128)S(1)}, u32[]{:S(2)}, u32[]{:S(2)}) %collective-permute-start.5) | collective-permute-done | bytes 544 | tf_op jit(solution)/shard_map/rows/ppermute | solution.py:126
  51.6 24.5 %all-gather.3.cloned.1.call-done = bf16[1024,1152]{0,1:T(8,128)(2,1)} async-done(((bf16[128,1152]{0,1:T(8,128)(2,1)}), bf16[1024,1152]{0,1:T(8,128)(2,1)}) %all-gather.3.cloned.1.call-update) | async-done | bytes 2359312 | tf_op jit(solution)/shard_map/weights/all_gather | solution.py:205
  77.0 2.6 add_convert_fusion.qkv_ref
  79.6 6.2 %attend.1 = bf16[512,256]{1,0:T(8,128)(2,1)S(1)} custom-call(bf16[512,768]{1,0:T(8,128)(2,1)S(1)} %add_convert_fusion.qkv_ref, f32[512,128]{1,0:T(8,128)S(1)} %fusion.70.mask_ref), custom_call_target="tpu_custom_call" | custom-call | tf_op jit(solution)/shard_map/forward/attend/pallas_call | solution.py:99
  90.5 4.9 collective-permute-done.8
  96.6 4.1 collective-permute-done.6
  112.4 5.5 %collective-permute-done.10 = bf16[128,1024]{1,0:T(8,128)(2,1)} collective-permute-done((bf16[128,1024]{1,0:T(8,128)(2,1)}, bf16[128,1024]{1,0:T(8,128)(2,1)}, u32[]{:S(2)}, u32[]{:S(2)}) %collective-permute-start.10) | collective-permute-done | bytes 262176 | tf_op jit(solution)/shard_map/forward/ppermute | solution.py:126
  117.9 32.1 %all-gather.5.cloned.1.call-done = bf16[1024,2048]{1,0:T(8,128)(2,1)} async-done(((bf16[128,2048]{1,0:T(8,128)(2,1)}), bf16[1024,2048]{1,0:T(8,128)(2,1)}) %all-gather.5.cloned.1.call-update) | async-done | bytes 4194320 | tf_op jit(solution)/shard_map/weights/all_gather | solution.py:207
  150.0 3.3 fusion.12
  153.4 4.2 convert_reduce_fusion.1
  164.2 2.8 collective-permute-done.20
  168.2 4.6 collective-permute-done.18
  173.2 5.0 collective-permute-done.14
  179.5 4.0 collective-permute-done.12
  188.6 6.1 %collective-permute-done.23 = bf16[128,1024]{1,0:T(8,128)(2,1)S(1)} collective-permute-done((bf16[128,1024]{1,0:T(8,128)(2,1)}, bf16[128,1024]{1,0:T(8,128)(2,1)S(1)}, u32[]{:S(2)}, u32[]{:S(2)}) %collective-permute-start.23) | collective-permute-done | bytes 262176 | tf_op jit(solution)/shard_map/backward/ppermute | solution.py:126
  194.6 6.2 %collective-permute-done.22 = bf16[128,1024]{1,0:T(8,128)(2,1)} collective-permute-done((bf16[128,1024]{1,0:T(8,128)(2,1)}, bf16[128,1024]{1,0:T(8,128)(2,1)}, u32[]{:S(2)}, u32[]{:S(2)}) %collective-permute-start.22) | collective-permute-done | bytes 262176 | tf_op jit(solution)/shard_map/backward/ppermute | solution.py:126
  202.6 8.3 %attend_back.1 = bf16[512,768]{1,0:T(8,128)(2,1)S(1)} custom-call(bf16[512,768]{1,0:T(8,128)(2,1)S(1)} %add_convert_fusion.qkv_ref, f32[512,128]{1,0:T(8,128)S(1)} %fusion.70.mask_ref, bf16[512,256]{1,0:T(8,128)(2,1)S(1)} %convolution_convert_fusion.grad_ref), custom_call_target="tpu_custom_call" | custom-call | tf_op jit(solution)/shard_map/backward/attend_back/pallas_call | solution.py:99
  215.1 2.9 fusion.91
  221.3 4.0 collective-permute-done.24
  225.8 4.7 select_maximum_fusion
  231.8 2.6 fusion.72
  234.4 2.7 fusion.71
  237.1 4.1 pad_maximum_fusion
  242.2 82.9 %reduce-scatter.3.cloned.1.call-done = f32[128,1152]{0,1:T(8,128)} async-done(((f32[1024,1152]{0,1:T(8,128)}), f32[128,1152]{0,1:T(8,128)}) %reduce-scatter.3.cloned.1.call-update) | async-done | bytes 589840 | tf_op jit(solution)/shard_map/attention_sums/reduce_scatter | solution.py:307
  327.2 3.7 all-to-all-start.2
  332.0 8.2 %all-to-all-done.2 = f32[4,32,1152]{2,1,0:T(8,128)S(1)} async-done(((f32[4,32,1152]{2,1,0:T(8,128)}), f32[4,32,1152]{2,1,0:T(8,128)S(1)}, u32[]{:S(2)}, u32[]{:S(2)}) %all-to-all-start.2) | async-done | bytes 589856 | tf_op jit(solution)/shard_map/owners/all_to_all | solution.py:141
  346.3 131.5 %reduce-scatter.5.cloned.1.call-done = f32[128,2048]{0,1:T(8,128)} async-done(((f32[1024,2048]{0,1:T(8,128)}), f32[128,2048]{0,1:T(8,128)}) %reduce-scatter.5.cloned.1.call-update) | async-done | bytes 1048592 | tf_op jit(solution)/shard_map/branch_sums/reduce_scatter | solution.py:256
  477.8 2.5 copy.117
  480.3 3.5 all-to-all-start.3
  486.5 11.8 %all-to-all-done.3 = f32[4,32,2048]{2,1,0:T(8,128)S(1)} async-done(((f32[4,32,2048]{2,1,0:T(8,128)}), f32[4,32,2048]{2,1,0:T(8,128)S(1)}, u32[]{:S(2)}, u32[]{:S(2)}) %all-to-all-start.3) | async-done | bytes 1048608 | tf_op jit(solution)/shard_map/owners/all_to_all | solution.py:141
  (241 shorter events, 85.1 us)
Async XLA Ops:
  7.2 69.0 %all-gather.3.cloned.1.call-start = ((), (), s32[]{:S(2)}) async-start(), calls=%async_computation.6 | async-start | bytes 2654208 | tf_op jit(solution)/shard_map/weights/all_gather | solution.py:205
  21.9 128.1 %all-gather.5.cloned.1.call-start = ((), (), s32[]{:S(2)}) async-start(), calls=%async_computation.7 | async-start | bytes 4718592 | tf_op jit(solution)/shard_map/weights/all_gather | solution.py:207
  35.0 290.1 %reduce-scatter.3.cloned.1.call-start = ((), (), s32[]{:S(2)}) async-start(), calls=%async_computation.8 | async-start | bytes 5308416 | tf_op jit(solution)/shard_map/attention_sums/reduce_scatter | solution.py:307
  35.1 15.8 %collective-permute-start.2 = (bf16[128,1024]{1,0:T(8,128)(2,1)S(1)}, bf16[128,1024]{1,0:T(8,128)(2,1)S(1)}, u32[]{:S(2)}, u32[]{:S(2)}) collective-permute-start(bf16[128,1024]{1,0:T(8,128)(2,1)S(1)} %copy-done), channel_id=1, source_target_pairs={{0,3},{1,0},{2,1},{3,2},{4,7},{5,4},{6,5},{7,6},{8,11},{9,8},{10,9... | collective-permute-start | bytes 786440 | tf_op jit(solution)/shard_map/rows/ppermute | solution.py:126
  35.2 15.8 %collective-permute-start.1 = (bf16[128,1024]{1,0:T(8,128)(2,1)S(1)}, bf16[128,1024]{1,0:T(8,128)(2,1)S(1)}, u32[]{:S(2)}, u32[]{:S(2)}) collective-permute-start(bf16[128,1024]{1,0:T(8,128)(2,1)S(1)} %copy-done), channel_id=1, source_target_pairs={{0,2},{1,3},{2,0},{3,1},{4,6},{5,7},{6,4},{7,5},{8,10},{9,11},{10,... | collective-permute-start | bytes 786440 | tf_op jit(solution)/shard_map/rows/ppermute | solution.py:126
  36.5 14.4 %collective-permute-start = (bf16[128,1024]{1,0:T(8,128)(2,1)S(1)}, bf16[128,1024]{1,0:T(8,128)(2,1)S(1)}, u32[]{:S(2)}, u32[]{:S(2)}) collective-permute-start(bf16[128,1024]{1,0:T(8,128)(2,1)S(1)} %copy-done), channel_id=1, source_target_pairs={{0,1},{1,2},{2,3},{3,0},{4,5},{5,6},{6,7},{7,4},{8,9},{9,10},{10,1... | collective-permute-start | bytes 786440 | tf_op jit(solution)/shard_map/rows/ppermute | solution.py:126
  37.3 10.1 %collective-permute-start.5 = (s32[128]{0:T(128)S(1)}, s32[128]{0:T(128)S(1)}, u32[]{:S(2)}, u32[]{:S(2)}) collective-permute-start(s32[128]{0:T(128)S(1)} %subtract_select_fusion.1), channel_id=1, source_target_pairs={{0,3},{1,0},{2,1},{3,2},{4,7},{5,4},{6,5},{7,6},{8,11},{9,8},{10,9... | collective-permute-start | bytes 1544 | tf_op jit(solution)/shard_map/rows/ppermute | solution.py:126
  39.1 10.2 %collective-permute-start.4 = (s32[128]{0:T(128)S(1)}, s32[128]{0:T(128)S(1)}, u32[]{:S(2)}, u32[]{:S(2)}) collective-permute-start(s32[128]{0:T(128)S(1)} %subtract_select_fusion.1), channel_id=1, source_target_pairs={{0,2},{1,3},{2,0},{3,1},{4,6},{5,7},{6,4},{7,5},{8,10},{9,11},{10,... | collective-permute-start | bytes 1544 | tf_op jit(solution)/shard_map/rows/ppermute | solution.py:126
  87.4 8.0 %collective-permute-start.8 = (bf16[128,1024]{1,0:T(8,128)(2,1)S(1)}, bf16[128,1024]{1,0:T(8,128)(2,1)S(1)}, u32[]{:S(2)}, u32[]{:S(2)}) collective-permute-start(bf16[128,1024]{1,0:T(8,128)(2,1)S(1)} %get-tuple-element.156), channel_id=1, source_target_pairs={{0,1},{1,2},{2,3},{3,0},{4,5},{5,6},{6,7},{7,4},{8,9},{9,10},{10,1... | collective-permute-start | bytes 786440 | tf_op jit(solution)/shard_map/forward/ppermute | solution.py:136
  87.4 9.2 %collective-permute-start.7 = (bf16[128,1024]{1,0:T(8,128)(2,1)S(1)}, bf16[128,1024]{1,0:T(8,128)(2,1)S(1)}, u32[]{:S(2)}, u32[]{:S(2)}) collective-permute-start(bf16[128,1024]{1,0:T(8,128)(2,1)S(1)} %get-tuple-element.157), channel_id=1, source_target_pairs={{0,2},{1,3},{2,0},{3,1},{4,6},{5,7},{6,4},{7,5},{8,10},{9,11},{10,... | collective-permute-start | bytes 786440 | tf_op jit(solution)/shard_map/forward/ppermute | solution.py:136
  89.0 11.7 %collective-permute-start.6 = (bf16[128,1024]{1,0:T(8,128)(2,1)S(1)}, bf16[128,1024]{1,0:T(8,128)(2,1)S(1)}, u32[]{:S(2)}, u32[]{:S(2)}) collective-permute-start(bf16[128,1024]{1,0:T(8,128)(2,1)S(1)} %get-tuple-element.155), channel_id=1, source_target_pairs={{0,3},{1,0},{2,1},{3,2},{4,7},{5,4},{6,5},{7,6},{8,11},{9,8},{10,9... | collective-permute-start | bytes 786440 | tf_op jit(solution)/shard_map/forward/ppermute | solution.py:136
  102.1 9.3 %collective-permute-start.11 = (bf16[128,1024]{1,0:T(8,128)(2,1)}, bf16[128,1024]{1,0:T(8,128)(2,1)}, u32[]{:S(2)}, u32[]{:S(2)}) collective-permute-start(bf16[128,1024]{1,0:T(8,128)(2,1)} %add_convert_fusion.1), channel_id=1, source_target_pairs={{0,3},{1,0},{2,1},{3,2},{4,7},{5,4},{6,5},{7,6},{8,11},{9,8},{10,9... | collective-permute-start | bytes 786440 | tf_op jit(solution)/shard_map/forward/ppermute | solution.py:126
  104.4 13.5 %collective-permute-start.10 = (bf16[128,1024]{1,0:T(8,128)(2,1)}, bf16[128,1024]{1,0:T(8,128)(2,1)}, u32[]{:S(2)}, u32[]{:S(2)}) collective-permute-start(bf16[128,1024]{1,0:T(8,128)(2,1)} %add_convert_fusion.1), channel_id=1, source_target_pairs={{0,2},{1,3},{2,0},{3,1},{4,6},{5,7},{6,4},{7,5},{8,10},{9,11},{10,... | collective-permute-start | bytes 786440 | tf_op jit(solution)/shard_map/forward/ppermute | solution.py:126
  104.9 13.0 %collective-permute-start.9 = (bf16[128,1024]{1,0:T(8,128)(2,1)}, bf16[128,1024]{1,0:T(8,128)(2,1)}, u32[]{:S(2)}, u32[]{:S(2)}) collective-permute-start(bf16[128,1024]{1,0:T(8,128)(2,1)} %add_convert_fusion.1), channel_id=1, source_target_pairs={{0,1},{1,2},{2,3},{3,0},{4,5},{5,6},{6,7},{7,4},{8,9},{9,10},{10,1... | collective-permute-start | bytes 786440 | tf_op jit(solution)/shard_map/forward/ppermute | solution.py:126
  105.8 47.6 %collective-permute-start.17 = (bf16[128,1024]{1,0:T(8,128)(2,1)}, bf16[128,1024]{1,0:T(8,128)(2,1)}, u32[]{:S(2)}, u32[]{:S(2)}) collective-permute-start(bf16[128,1024]{1,0:T(8,128)(2,1)} %get-tuple-element.128), channel_id=1, source_target_pairs={{0,3},{1,0},{2,1},{3,2},{4,7},{5,4},{6,5},{7,6},{8,11},{9,8},{10,9... | collective-permute-start | bytes 786440 | tf_op jit(solution)/shard_map/rows/ppermute | solution.py:126
  107.5 45.9 %collective-permute-start.16 = (bf16[128,1024]{1,0:T(8,128)(2,1)}, bf16[128,1024]{1,0:T(8,128)(2,1)}, u32[]{:S(2)}, u32[]{:S(2)}) collective-permute-start(bf16[128,1024]{1,0:T(8,128)(2,1)} %get-tuple-element.128), channel_id=1, source_target_pairs={{0,2},{1,3},{2,0},{3,1},{4,6},{5,7},{6,4},{7,5},{8,10},{9,11},{10,... | collective-permute-start | bytes 786440 | tf_op jit(solution)/shard_map/rows/ppermute | solution.py:126
  111.4 42.0 %collective-permute-start.15 = (bf16[128,1024]{1,0:T(8,128)(2,1)}, bf16[128,1024]{1,0:T(8,128)(2,1)}, u32[]{:S(2)}, u32[]{:S(2)}) collective-permute-start(bf16[128,1024]{1,0:T(8,128)(2,1)} %get-tuple-element.128), channel_id=1, source_target_pairs={{0,1},{1,2},{2,3},{3,0},{4,5},{5,6},{6,7},{7,4},{8,9},{9,10},{10,1... | collective-permute-start | bytes 786440 | tf_op jit(solution)/shard_map/rows/ppermute | solution.py:126
  159.0 8.0 %collective-permute-start.20 = (bf16[128,1024]{1,0:T(8,128)(2,1)S(1)}, bf16[128,1024]{1,0:T(8,128)(2,1)S(1)}, u32[]{:S(2)}, u32[]{:S(2)}) collective-permute-start(bf16[128,1024]{1,0:T(8,128)(2,1)S(1)} %get-tuple-element.150), channel_id=1, source_target_pairs={{0,1},{1,2},{2,3},{3,0},{4,5},{5,6},{6,7},{7,4},{8,9},{9,10},{10,1... | collective-permute-start | bytes 786440 | tf_op jit(solution)/shard_map/branch/ppermute | solution.py:136
  159.0 9.2 %collective-permute-start.19 = (bf16[128,1024]{1,0:T(8,128)(2,1)S(1)}, bf16[128,1024]{1,0:T(8,128)(2,1)S(1)}, u32[]{:S(2)}, u32[]{:S(2)}) collective-permute-start(bf16[128,1024]{1,0:T(8,128)(2,1)S(1)} %get-tuple-element.151), channel_id=1, source_target_pairs={{0,2},{1,3},{2,0},{3,1},{4,6},{5,7},{6,4},{7,5},{8,10},{9,11},{10,... | collective-permute-start | bytes 786440 | tf_op jit(solution)/shard_map/branch/ppermute | solution.py:136
  160.5 12.3 %collective-permute-start.18 = (bf16[128,1024]{1,0:T(8,128)(2,1)S(1)}, bf16[128,1024]{1,0:T(8,128)(2,1)S(1)}, u32[]{:S(2)}, u32[]{:S(2)}) collective-permute-start(bf16[128,1024]{1,0:T(8,128)(2,1)S(1)} %get-tuple-element.149), channel_id=1, source_target_pairs={{0,3},{1,0},{2,1},{3,2},{4,7},{5,4},{6,5},{7,6},{8,11},{9,8},{10,9... | collective-permute-start | bytes 786440 | tf_op jit(solution)/shard_map/branch/ppermute | solution.py:136
  163.5 14.7 %collective-permute-start.14 = (bf16[128,1024]{1,0:T(8,128)(2,1)S(1)}, bf16[128,1024]{1,0:T(8,128)(2,1)S(1)}, u32[]{:S(2)}, u32[]{:S(2)}) collective-permute-start(bf16[128,1024]{1,0:T(8,128)(2,1)S(1)} %get-tuple-element.153), channel_id=1, source_target_pairs={{0,1},{1,2},{2,3},{3,0},{4,5},{5,6},{6,7},{7,4},{8,9},{9,10},{10,1... | collective-permute-start | bytes 786440 | tf_op jit(solution)/shard_map/result/ppermute | solution.py:136
  163.6 15.9 %collective-permute-start.13 = (bf16[128,1024]{1,0:T(8,128)(2,1)S(1)}, bf16[128,1024]{1,0:T(8,128)(2,1)S(1)}, u32[]{:S(2)}, u32[]{:S(2)}) collective-permute-start(bf16[128,1024]{1,0:T(8,128)(2,1)S(1)} %get-tuple-element.154), channel_id=1, source_target_pairs={{0,2},{1,3},{2,0},{3,1},{4,6},{5,7},{6,4},{7,5},{8,10},{9,11},{10,... | collective-permute-start | bytes 786440 | tf_op jit(solution)/shard_map/result/ppermute | solution.py:136
  167.0 16.4 %collective-permute-start.12 = (bf16[128,1024]{1,0:T(8,128)(2,1)S(1)}, bf16[128,1024]{1,0:T(8,128)(2,1)S(1)}, u32[]{:S(2)}, u32[]{:S(2)}) collective-permute-start(bf16[128,1024]{1,0:T(8,128)(2,1)S(1)} %get-tuple-element.152), channel_id=1, source_target_pairs={{0,3},{1,0},{2,1},{3,2},{4,7},{5,4},{6,5},{7,6},{8,11},{9,8},{10,9... | collective-permute-start | bytes 786440 | tf_op jit(solution)/shard_map/result/ppermute | solution.py:136
  185.7 8.9 %collective-permute-start.23 = (bf16[128,1024]{1,0:T(8,128)(2,1)}, bf16[128,1024]{1,0:T(8,128)(2,1)S(1)}, u32[]{:S(2)}, u32[]{:S(2)}) collective-permute-start(bf16[128,1024]{1,0:T(8,128)(2,1)} %get-tuple-element.130), channel_id=1, source_target_pairs={{0,3},{1,0},{2,1},{3,2},{4,7},{5,4},{6,5},{7,6},{8,11},{9,8},{10,9... | collective-permute-start | bytes 786440 | tf_op jit(solution)/shard_map/backward/ppermute | solution.py:126
  187.7 13.1 %collective-permute-start.22 = (bf16[128,1024]{1,0:T(8,128)(2,1)}, bf16[128,1024]{1,0:T(8,128)(2,1)}, u32[]{:S(2)}, u32[]{:S(2)}) collective-permute-start(bf16[128,1024]{1,0:T(8,128)(2,1)} %get-tuple-element.130), channel_id=1, source_target_pairs={{0,2},{1,3},{2,0},{3,1},{4,6},{5,7},{6,4},{7,5},{8,10},{9,11},{10,... | collective-permute-start | bytes 786440 | tf_op jit(solution)/shard_map/backward/ppermute | solution.py:126
  188.2 12.6 %collective-permute-start.21 = (bf16[128,1024]{1,0:T(8,128)(2,1)}, bf16[128,1024]{1,0:T(8,128)(2,1)}, u32[]{:S(2)}, u32[]{:S(2)}) collective-permute-start(bf16[128,1024]{1,0:T(8,128)(2,1)} %get-tuple-element.130), channel_id=1, source_target_pairs={{0,1},{1,2},{2,3},{3,0},{4,5},{5,6},{6,7},{7,4},{8,9},{9,10},{10,1... | collective-permute-start | bytes 786440 | tf_op jit(solution)/shard_map/backward/ppermute | solution.py:126
  212.1 8.0 %collective-permute-start.26 = (bf16[128,1024]{1,0:T(8,128)(2,1)S(1)}, bf16[128,1024]{1,0:T(8,128)(2,1)S(1)}, u32[]{:S(2)}, u32[]{:S(2)}) collective-permute-start(bf16[128,1024]{1,0:T(8,128)(2,1)S(1)} %get-tuple-element.147), channel_id=1, source_target_pairs={{0,1},{1,2},{2,3},{3,0},{4,5},{5,6},{6,7},{7,4},{8,9},{9,10},{10,1... | collective-permute-start | bytes 786440 | tf_op jit(solution)/shard_map/backward/ppermute | solution.py:136
  212.1 9.2 %collective-permute-start.25 = (bf16[128,1024]{1,0:T(8,128)(2,1)S(1)}, bf16[128,1024]{1,0:T(8,128)(2,1)S(1)}, u32[]{:S(2)}, u32[]{:S(2)}) collective-permute-start(bf16[128,1024]{1,0:T(8,128)(2,1)S(1)} %get-tuple-element.148), channel_id=1, source_target_pairs={{0,2},{1,3},{2,0},{3,1},{4,6},{5,7},{6,4},{7,5},{8,10},{9,11},{10,... | collective-permute-start | bytes 786440 | tf_op jit(solution)/shard_map/backward/ppermute | solution.py:136
  213.7 11.7 %collective-permute-start.24 = (bf16[128,1024]{1,0:T(8,128)(2,1)S(1)}, bf16[128,1024]{1,0:T(8,128)(2,1)S(1)}, u32[]{:S(2)}, u32[]{:S(2)}) collective-permute-start(bf16[128,1024]{1,0:T(8,128)(2,1)S(1)} %get-tuple-element.146), channel_id=1, source_target_pairs={{0,3},{1,0},{2,1},{3,2},{4,7},{5,4},{6,5},{7,6},{8,11},{9,8},{10,9... | collective-permute-start | bytes 786440 | tf_op jit(solution)/shard_map/backward/ppermute | solution.py:136
  230.6 247.2 %reduce-scatter.5.cloned.1.call-start = ((), (), s32[]{:S(2)}) async-start(), calls=%async_computation.9 | async-start | bytes 9437184 | tf_op jit(solution)/shard_map/branch_sums/reduce_scatter | solution.py:256
  327.2 13.0 %all-to-all-start.2 = ((f32[4,32,1152]{2,1,0:T(8,128)}), f32[4,32,1152]{2,1,0:T(8,128)S(1)}, u32[]{:S(2)}, u32[]{:S(2)}) async-start(f32[4,32,1152]{2,1,0:T(8,128)} %bitcast.35), calls=%async_computation.3 | async-start | bytes 1179648 | tf_op jit(solution)/shard_map/owners/all_to_all | solution.py:141
  480.3 18.0 %all-to-all-start.3 = ((f32[4,32,2048]{2,1,0:T(8,128)}), f32[4,32,2048]{2,1,0:T(8,128)S(1)}, u32[]{:S(2)}, u32[]{:S(2)}) async-start(f32[4,32,2048]{2,1,0:T(8,128)} %bitcast.38), calls=%async_computation.5 | async-start | bytes 2097152 | tf_op jit(solution)/shard_map/owners/all_to_all | solution.py:141
  (32 other events, 446.4 us)
Sparse Core Ops, SparseCore 0:
  22.0 54.0 all-gather.2
  78.3 71.6 all-gather.4
  230.7 94.3 reduce-scatter.2
  328.6 149.1 reduce-scatter.4

commit v2 on v1

--- a/solution.py
+++ b/solution.py
@@ -251,8 +251,10 @@
 
     with jax.named_scope("branch_sums"):
         branch_grads = jnp.concatenate(
-            [dot(second_in, grad_hidden, TN), dot(all_branch, active, TN)], axis=1
-        )
+            [dot(second_in, grad_hidden, TN).astype(BF), dot(all_branch, active, TN).astype(BF)],
+            axis=1,
+        )
+        branch_grads, second_terms = lax.optimization_barrier((branch_grads, second_terms))
         branch_total = lax.psum_scatter(branch_grads, "dp", scatter_dimension=0, tiled=True)
 
     with jax.named_scope("backward"):
@@ -298,17 +300,18 @@
         vector_sums = jnp.concatenate([vector_sums, hidden_rows], axis=0)
         attention_grads = jnp.concatenate(
             [
-                dot(first_in, grad_qkv, TN),
-                dot(all_attn, attended, TN),
-                jnp.pad(vector_sums.T, ((0, 0), (0, VEC_PAD - vectors.shape[0]))),
+                dot(first_in, grad_qkv, TN).astype(BF),
+                dot(all_attn, attended, TN).astype(BF),
+                jnp.pad(vector_sums.T, ((0, 0), (0, VEC_PAD - vectors.shape[0]))).astype(BF),
             ],
             axis=1,
         )
+        attention_grads, branch_total = lax.optimization_barrier((attention_grads, branch_total))
         attention_total = lax.psum_scatter(attention_grads, "dp", scatter_dimension=0, tiled=True)
 
     with jax.named_scope("owners"):
-        branch_parts = exchange(branch_total.reshape(ways, rows_own, -1))
-        attention_parts = exchange(attention_total.reshape(ways, rows_own, -1))
+        branch_parts = exchange(branch_total.reshape(ways, rows_own, -1)).astype(F32)
+        attention_parts = exchange(attention_total.reshape(ways, rows_own, -1)).astype(F32)
         qkv_total = (
             attention_parts[:, :, : 3 * width]
             .reshape(ways, rows_own, 3, width)

time: 520 us -> 372 us (0.72)
  waiting for transfers between devices: 355 us -> 215 us
  starting transfers between devices: 32.4 us -> 25 us
  other arithmetic: 30.6 us -> 24.4 us
    reduce_scatter x1 -> x0, waiting for transfers between devices: 131 us -> none  [per_device(): lax.psum_scatter(branch_grads, 'dp', scatter_dimension=0, tiled=True)]
    reduce_scatter x1, waiting for transfers between devices: 82.9 us -> 54 us  [per_device(): lax.psum_scatter(attention_grads, 'dp', scatter_dimension=0, tiled=True)]
    unnamed x4 -> x5, waiting for transfers between devices: 0.07 us -> 24.5 us
    all_to_all x2, waiting for transfers between devices: 20 us -> 9.16 us  [exchange(): lax.all_to_all(values, 'fsdp', split_axis=0, concat_axis=0, tiled=True)]
    unnamed x70 -> x84, local copies, waits for them, and re-layouts: 3.78 us -> 12.3 us
    ppermute x15, starting transfers between devices: 15.3 us -> 9.75 us  [gather_rows(): pieces.append(lax.ppermute(values, 'fsdp', order))]
  transfers between devices with their start and end apart: 33 -> 33, of which waited for: 24 -> 22; matrix products, arithmetic and copies ran while one was open for 8% -> 14% of each run, Pallas kernels for 1% -> 4%
where the time goes in v2:
time: 372 us; the launch traced here: 371 us
  waiting for transfers between devices  215 us (58%)
  matrix products  28.7 us (8%)
  local copies, waits for them, and re-layouts  26.7 us (7%)
  starting transfers between devices  25 us (7%)
  other arithmetic  24.4 us (7%)
  blocking collectives  22.3 us (6%)
  between operations  14.8 us (4%)
  Pallas kernels  14.5 us (4%)
    reduce_scatter x1, waiting for transfers between devices, per_device(): lax.psum_scatter(attention_grads, 'dp', scatter_dimension=0, tiled=True)  54 us
    ppermute x12, waiting for transfers between devices, sum_rows(): total = total + lax.ppermute(piece, 'fsdp', order).astype(F32)  37.3 us
    all_gather x1, waiting for transfers between devices, per_device(): second_weights = lax.all_gather(second_rows, 'dp', axis=0, tiled=True)  34.1 us
    ppermute x15, waiting for transfers between devices, gather_rows(): pieces.append(lax.ppermute(values, 'fsdp', order))  32.6 us
    dot_general x12, matrix products, dot(): return lax.dot_general(left, right, dims, preferred_element_type=F32)  28.7 us
    unnamed x5, waiting for transfers between devices  24.5 us
    all_gather x1, waiting for transfers between devices, per_device(): first_weights = lax.all_gather(first_rows, 'dp', axis=0, tiled=True)  23 us
    all_to_all x2, blocking collectives, exchange(): lax.all_to_all(values, 'fsdp', split_axis=0, concat_axis=0, tiled=True)  22.3 us
  transfers between devices with their start and end apart: 33, of which 22 were waited for; matrix products, arithmetic and copies ran while one was open for 14% of the time, Pallas kernels for 4%

profile of v2, /device:TPU:0, one launch (start us, length us, event | category | flops | bytes accessed | tf_op | source)
XLA Modules:
  0.0 370.9 jit_solution(5071064785654093198)
XLA Ops:
  9.9 10.4 %all_to_all.20 = bf16[4,32,1152]{2,1,0:T(8,128)(2,1)S(1)} all-to-all(bf16[4,32,1152]{2,1,0:T(8,128)(2,1)S(1)} %pad_maximum_fusion.9), channel_id=1, replica_groups=mesh['dp'=8,'fsdp'=4] {'fsdp'}, dimensions={0} | all-to-all | bytes 589824 | tf_op jit(solution)/shard_map/weights/all_to_all | solution.py:141
  22.4 11.9 %all_to_all.21 = bf16[4,32,2048]{2,1,0:T(8,128)(2,1)} all-to-all(bf16[4,32,2048]{2,1,0:T(8,128)(2,1)S(1)} %copy.113), channel_id=1, replica_groups=mesh['dp'=8,'fsdp'=4] {'fsdp'}, dimensions={0} | all-to-all | bytes 1048576 | tf_op jit(solution)/shard_map/weights/all_to_all | solution.py:141
  39.1 9.6 %collective-permute-done.4 = s32[128]{0:T(128)S(1)} collective-permute-done((s32[128]{0:T(128)S(1)}, s32[128]{0:T(128)S(1)}, u32[]{:S(2)}, u32[]{:S(2)}) %collective-permute-start.4) | collective-permute-done | bytes 544 | tf_op jit(solution)/shard_map/rows/ppermute | solution.py:126
  48.7 3.0 collective-permute-done.3
  52.5 23.0 %all-gather.3.cloned.1.call-done = bf16[1024,1152]{0,1:T(8,128)(2,1)} async-done(((bf16[128,1152]{0,1:T(8,128)(2,1)}), bf16[1024,1152]{0,1:T(8,128)(2,1)}) %all-gather.3.cloned.1.call-update) | async-done | bytes 2359312 | tf_op jit(solution)/shard_map/weights/all_gather | solution.py:205
  76.3 2.6 add_convert_fusion.qkv_ref
  78.9 6.2 %attend.1 = bf16[512,256]{1,0:T(8,128)(2,1)S(1)} custom-call(bf16[512,768]{1,0:T(8,128)(2,1)S(1)} %add_convert_fusion.qkv_ref, f32[512,128]{1,0:T(8,128)S(1)} %fusion.72.mask_ref), custom_call_target="tpu_custom_call" | custom-call | tf_op jit(solution)/shard_map/forward/attend/pallas_call | solution.py:99
  88.6 4.8 %collective-permute-done.6 = bf16[128,1024]{1,0:T(8,128)(2,1)S(1)} collective-permute-done((bf16[128,1024]{1,0:T(8,128)(2,1)S(1)}, bf16[128,1024]{1,0:T(8,128)(2,1)S(1)}, u32[]{:S(2)}, u32[]{:S(2)}) %collective-permute-start.6) | collective-permute-done | bytes 262176 | tf_op jit(solution)/shard_map/forward/ppermute | solution.py:136
  93.4 7.6 %collective-permute-done.7 = bf16[128,1024]{1,0:T(8,128)(2,1)S(1)} collective-permute-done((bf16[128,1024]{1,0:T(8,128)(2,1)S(1)}, bf16[128,1024]{1,0:T(8,128)(2,1)S(1)}, u32[]{:S(2)}, u32[]{:S(2)}) %collective-permute-start.7) | collective-permute-done | bytes 262176 | tf_op jit(solution)/shard_map/forward/ppermute | solution.py:136
  105.2 6.0 %collective-permute-done.10 = bf16[128,1024]{1,0:T(8,128)(2,1)} collective-permute-done((bf16[128,1024]{1,0:T(8,128)(2,1)S(1)}, bf16[128,1024]{1,0:T(8,128)(2,1)}, u32[]{:S(2)}, u32[]{:S(2)}) %collective-permute-start.10) | collective-permute-done | bytes 262176 | tf_op jit(solution)/shard_map/forward/ppermute | solution.py:126
  111.2 4.0 %collective-permute-done.11 = bf16[128,1024]{1,0:T(8,128)(2,1)} collective-permute-done((bf16[128,1024]{1,0:T(8,128)(2,1)S(1)}, bf16[128,1024]{1,0:T(8,128)(2,1)}, u32[]{:S(2)}, u32[]{:S(2)}) %collective-permute-start.11) | collective-permute-done | bytes 262176 | tf_op jit(solution)/shard_map/forward/ppermute | solution.py:126
  115.2 34.1 %all-gather.5.cloned.1.call-done = bf16[1024,2048]{1,0:T(8,128)(2,1)} async-done(((bf16[128,2048]{1,0:T(8,128)(2,1)}), bf16[1024,2048]{1,0:T(8,128)(2,1)}) %all-gather.5.cloned.1.call-update) | async-done | bytes 4194320 | tf_op jit(solution)/shard_map/weights/all_gather | solution.py:207
  149.3 3.2 fusion.14
  152.6 3.9 %convert_reduce_fusion.1 = (bf16[1024]{0:T(1024)(128)(2,1)S(1)}, bf16[512,1024]{1,0:T(8,128)(2,1)S(1)}) fusion(f32[512,1024]{1,0:T(8,128)S(1)} %fusion.14, f32[1024]{0:T(1024)S(1)} %dynamic_slice.17, bf16[1024,2048]{1,0:T(8,128)(2,1)S(1)} %copy-done.27, bf16[128,1024]{1,0:T(8,128)(2,1)} %collective-permute-done.17, ...), kind=kOutput, calls=%fused_computation.12 | convolution fusion | flops 1088945152 | bytes 6297600 | tf_op jit(solution)/shard_map/branch/dot_general | solution.py:33
  162.0 2.7 convolution_convert_fusion
  164.7 2.4 pad_maximum_fusion
  167.2 4.9 %collective-permute-done.19 = bf16[128,1024]{1,0:T(8,128)(2,1)S(1)} collective-permute-done((bf16[128,1024]{1,0:T(8,128)(2,1)S(1)}, bf16[128,1024]{1,0:T(8,128)(2,1)S(1)}, u32[]{:S(2)}, u32[]{:S(2)}) %collective-permute-start.19) | collective-permute-done | bytes 262176 | tf_op jit(solution)/shard_map/branch/ppermute | solution.py:136
  172.3 6.6 %copy.132 = bf16[1024,2048]{1,0:T(8,128)(2,1)} copy(bf16[1024,2048]{0,1:T(8,128)(2,1)} %pad_maximum_fusion) | data formatting | bytes 8388608
  178.9 3.7 %fusion.106 = (bf16[512,1024]{1,0:T(8,128)(2,1)S(1)}, f32[512,1024]{1,0:T(8,128)S(1)}) fusion(bf16[1024,2048]{1,0:T(8,128)(2,1)} %all-gather.5.cloned.1.call-done, f32[512,1024]{1,0:T(8,128)} %copy-done.36, f32[1024]{0:T(1024)S(1)} %dynamic_slice.17), kind=kOutput, calls=%fused_computation.213 | convolution fusion | flops 1079508992 | bytes 7344128 | tf_op jit(solution)/shard_map/result/dot_general | solution.py:33
  183.5 5.8 %collective-permute-done.12 = bf16[128,1024]{1,0:T(8,128)(2,1)S(1)} collective-permute-done((bf16[128,1024]{1,0:T(8,128)(2,1)S(1)}, bf16[128,1024]{1,0:T(8,128)(2,1)S(1)}, u32[]{:S(2)}, u32[]{:S(2)}) %collective-permute-start.12) | collective-permute-done | bytes 262176 | tf_op jit(solution)/shard_map/result/ppermute | solution.py:136
  189.3 5.7 %collective-permute-done.13 = bf16[128,1024]{1,0:T(8,128)(2,1)S(1)} collective-permute-done((bf16[128,1024]{1,0:T(8,128)(2,1)S(1)}, bf16[128,1024]{1,0:T(8,128)(2,1)S(1)}, u32[]{:S(2)}, u32[]{:S(2)}) %collective-permute-start.13) | collective-permute-done | bytes 262176 | tf_op jit(solution)/shard_map/result/ppermute | solution.py:136
  201.8 4.8 %collective-permute-done.21 = bf16[128,1024]{1,0:T(8,128)(2,1)S(1)} collective-permute-done((bf16[128,1024]{1,0:T(8,128)(2,1)}, bf16[128,1024]{1,0:T(8,128)(2,1)S(1)}, u32[]{:S(2)}, u32[]{:S(2)}) %collective-permute-start.21) | collective-permute-done | bytes 262176 | tf_op jit(solution)/shard_map/backward/ppermute | solution.py:126
  207.6 4.2 %collective-permute-done.23 = bf16[128,1024]{1,0:T(8,128)(2,1)S(1)} collective-permute-done((bf16[128,1024]{1,0:T(8,128)(2,1)}, bf16[128,1024]{1,0:T(8,128)(2,1)S(1)}, u32[]{:S(2)}, u32[]{:S(2)}) %collective-permute-start.23) | collective-permute-done | bytes 262176 | tf_op jit(solution)/shard_map/backward/ppermute | solution.py:126
  213.6 8.3 %attend_back.1 = bf16[512,768]{1,0:T(8,128)(2,1)S(1)} custom-call(bf16[512,768]{1,0:T(8,128)(2,1)S(1)} %add_convert_fusion.qkv_ref, f32[512,128]{1,0:T(8,128)S(1)} %fusion.72.mask_ref, bf16[512,256]{1,0:T(8,128)(2,1)S(1)} %convolution_convert_fusion.4.grad_ref), custom_call_target="tpu_custom_call" | custom-call | tf_op jit(solution)/shard_map/backward/attend_back/pallas_call | solution.py:99
  231.8 6.2 %collective-permute-done.25 = bf16[128,1024]{1,0:T(8,128)(2,1)S(1)} collective-permute-done((bf16[128,1024]{1,0:T(8,128)(2,1)S(1)}, bf16[128,1024]{1,0:T(8,128)(2,1)S(1)}, u32[]{:S(2)}, u32[]{:S(2)}) %collective-permute-start.25) | collective-permute-done | bytes 262176 | tf_op jit(solution)/shard_map/backward/ppermute | solution.py:136
  241.0 24.5 %reduce-scatter.7.cloned.1.call-done = bf16[128,2048]{1,0:T(8,128)(2,1)} async-done(((bf16[1024,2048]{1,0:T(8,128)(2,1)}), bf16[128,2048]{1,0:T(8,128)(2,1)}) %reduce-scatter.7.cloned.1.call-update) | async-done | bytes 524304
  269.6 4.1 %all-to-all-start.3 = ((bf16[4,32,2048]{2,1,0:T(8,128)(2,1)}), bf16[4,32,2048]{2,1,0:T(8,128)(2,1)}, u32[]{:S(2)}, u32[]{:S(2)}) async-start(bf16[4,32,2048]{2,1,0:T(8,128)(2,1)} %bitcast.150), calls=%async_computation.3 | async-start | bytes 1048576 | tf_op jit(solution)/shard_map/owners/all_to_all | solution.py:141
  274.0 2.5 copy.134
  278.8 3.8 %all-to-all-done.3 = bf16[4,32,2048]{2,1,0:T(8,128)(2,1)} async-done(((bf16[4,32,2048]{2,1,0:T(8,128)(2,1)}), bf16[4,32,2048]{2,1,0:T(8,128)(2,1)}, u32[]{:S(2)}, u32[]{:S(2)}) %all-to-all-start.3) | async-done | bytes 524320 | tf_op jit(solution)/shard_map/owners/all_to_all | solution.py:141
  293.3 54.0 %reduce-scatter.9.cloned.1.call-done = bf16[128,1152]{1,0:T(8,128)(2,1)} async-done(((bf16[1024,1152]{1,0:T(8,128)(2,1)}), bf16[128,1152]{1,0:T(8,128)(2,1)}) %reduce-scatter.9.cloned.1.call-update) | async-done | bytes 294928 | tf_op jit(solution)/shard_map/attention_sums/reduce_scatter | solution.py:310
  347.3 3.5 all-to-all-start.2
  351.8 5.3 %all-to-all-done.2 = bf16[4,32,1152]{2,1,0:T(8,128)(2,1)S(1)} async-done(((bf16[4,32,1152]{2,1,0:T(8,128)(2,1)}), bf16[4,32,1152]{2,1,0:T(8,128)(2,1)S(1)}, u32[]{:S(2)}, u32[]{:S(2)}) %all-to-all-start.2) | async-done | bytes 294944 | tf_op jit(solution)/shard_map/owners/all_to_all | solution.py:141
  (264 shorter events, 72.9 us)
Async XLA Ops:
  7.2 68.2 %all-gather.3.cloned.1.call-start = ((), (), s32[]{:S(2)}) async-start(), calls=%async_computation.6 | async-start | bytes 2654208 | tf_op jit(solution)/shard_map/weights/all_gather | solution.py:205
  21.2 128.0 %all-gather.5.cloned.1.call-start = ((), (), s32[]{:S(2)}) async-start(), calls=%async_computation.7 | async-start | bytes 4718592 | tf_op jit(solution)/shard_map/weights/all_gather | solution.py:207
  34.4 231.1 %reduce-scatter.7.cloned.1.call-start = ((), (), s32[]{:S(2)}) async-start(), calls=%async_computation.8 | async-start | bytes 4718592
  34.4 17.4 %collective-permute-start = (bf16[128,1024]{1,0:T(8,128)(2,1)S(1)}, bf16[128,1024]{1,0:T(8,128)(2,1)S(1)}, u32[]{:S(2)}, u32[]{:S(2)}) collective-permute-start(bf16[128,1024]{1,0:T(8,128)(2,1)S(1)} %copy-done), channel_id=1, source_target_pairs={{0,1},{1,2},{2,3},{3,0},{4,5},{5,6},{6,7},{7,4},{8,9},{9,10},{10,1... | collective-permute-start | bytes 786440 | tf_op jit(solution)/shard_map/rows/ppermute | solution.py:126
  34.5 17.3 %collective-permute-start.1 = (bf16[128,1024]{1,0:T(8,128)(2,1)S(1)}, bf16[128,1024]{1,0:T(8,128)(2,1)S(1)}, u32[]{:S(2)}, u32[]{:S(2)}) collective-permute-start(bf16[128,1024]{1,0:T(8,128)(2,1)S(1)} %copy-done), channel_id=1, source_target_pairs={{0,2},{1,3},{2,0},{3,1},{4,6},{5,7},{6,4},{7,5},{8,10},{9,11},{10,... | collective-permute-start | bytes 786440 | tf_op jit(solution)/shard_map/rows/ppermute | solution.py:126
  34.9 16.9 %collective-permute-start.2 = (bf16[128,1024]{1,0:T(8,128)(2,1)S(1)}, bf16[128,1024]{1,0:T(8,128)(2,1)S(1)}, u32[]{:S(2)}, u32[]{:S(2)}) collective-permute-start(bf16[128,1024]{1,0:T(8,128)(2,1)S(1)} %copy-done), channel_id=1, source_target_pairs={{0,3},{1,0},{2,1},{3,2},{4,7},{5,4},{6,5},{7,6},{8,11},{9,8},{10,9... | collective-permute-start | bytes 786440 | tf_op jit(solution)/shard_map/rows/ppermute | solution.py:126
  37.1 11.6 %collective-permute-start.4 = (s32[128]{0:T(128)S(1)}, s32[128]{0:T(128)S(1)}, u32[]{:S(2)}, u32[]{:S(2)}) collective-permute-start(s32[128]{0:T(128)S(1)} %subtract_select_fusion.1), channel_id=1, source_target_pairs={{0,2},{1,3},{2,0},{3,1},{4,6},{5,7},{6,4},{7,5},{8,10},{9,11},{10,... | collective-permute-start | bytes 1544 | tf_op jit(solution)/shard_map/rows/ppermute | solution.py:126
  38.7 9.9 %collective-permute-start.5 = (s32[128]{0:T(128)S(1)}, s32[128]{0:T(128)S(1)}, u32[]{:S(2)}, u32[]{:S(2)}) collective-permute-start(s32[128]{0:T(128)S(1)} %subtract_select_fusion.1), channel_id=1, source_target_pairs={{0,3},{1,0},{2,1},{3,2},{4,7},{5,4},{6,5},{7,6},{8,11},{9,8},{10,9... | collective-permute-start | bytes 1544 | tf_op jit(solution)/shard_map/rows/ppermute | solution.py:126
  86.6 6.8 %collective-permute-start.6 = (bf16[128,1024]{1,0:T(8,128)(2,1)S(1)}, bf16[128,1024]{1,0:T(8,128)(2,1)S(1)}, u32[]{:S(2)}, u32[]{:S(2)}) collective-permute-start(bf16[128,1024]{1,0:T(8,128)(2,1)S(1)} %get-tuple-element.162), channel_id=1, source_target_pairs={{0,3},{1,0},{2,1},{3,2},{4,7},{5,4},{6,5},{7,6},{8,11},{9,8},{10,9... | collective-permute-start | bytes 786440 | tf_op jit(solution)/shard_map/forward/ppermute | solution.py:136
  87.2 13.8 %collective-permute-start.7 = (bf16[128,1024]{1,0:T(8,128)(2,1)S(1)}, bf16[128,1024]{1,0:T(8,128)(2,1)S(1)}, u32[]{:S(2)}, u32[]{:S(2)}) collective-permute-start(bf16[128,1024]{1,0:T(8,128)(2,1)S(1)} %get-tuple-element.164), channel_id=1, source_target_pairs={{0,2},{1,3},{2,0},{3,1},{4,6},{5,7},{6,4},{7,5},{8,10},{9,11},{10,... | collective-permute-start | bytes 786440 | tf_op jit(solution)/shard_map/forward/ppermute | solution.py:136
  88.3 12.7 %collective-permute-start.8 = (bf16[128,1024]{1,0:T(8,128)(2,1)S(1)}, bf16[128,1024]{1,0:T(8,128)(2,1)S(1)}, u32[]{:S(2)}, u32[]{:S(2)}) collective-permute-start(bf16[128,1024]{1,0:T(8,128)(2,1)S(1)} %get-tuple-element.163), channel_id=1, source_target_pairs={{0,1},{1,2},{2,3},{3,0},{4,5},{5,6},{6,7},{7,4},{8,9},{9,10},{10,1... | collective-permute-start | bytes 786440 | tf_op jit(solution)/shard_map/forward/ppermute | solution.py:136
  101.7 9.4 %collective-permute-start.10 = (bf16[128,1024]{1,0:T(8,128)(2,1)S(1)}, bf16[128,1024]{1,0:T(8,128)(2,1)}, u32[]{:S(2)}, u32[]{:S(2)}) collective-permute-start(bf16[128,1024]{1,0:T(8,128)(2,1)S(1)} %add_convert_fusion.1), channel_id=1, source_target_pairs={{0,2},{1,3},{2,0},{3,1},{4,6},{5,7},{6,4},{7,5},{8,10},{9,11},{10,... | collective-permute-start | bytes 786440 | tf_op jit(solution)/shard_map/forward/ppermute | solution.py:126
  102.8 12.4 %collective-permute-start.11 = (bf16[128,1024]{1,0:T(8,128)(2,1)S(1)}, bf16[128,1024]{1,0:T(8,128)(2,1)}, u32[]{:S(2)}, u32[]{:S(2)}) collective-permute-start(bf16[128,1024]{1,0:T(8,128)(2,1)S(1)} %add_convert_fusion.1), channel_id=1, source_target_pairs={{0,3},{1,0},{2,1},{3,2},{4,7},{5,4},{6,5},{7,6},{8,11},{9,8},{10,9... | collective-permute-start | bytes 786440 | tf_op jit(solution)/shard_map/forward/ppermute | solution.py:126
  102.8 12.4 %collective-permute-start.9 = (bf16[128,1024]{1,0:T(8,128)(2,1)S(1)}, bf16[128,1024]{1,0:T(8,128)(2,1)}, u32[]{:S(2)}, u32[]{:S(2)}) collective-permute-start(bf16[128,1024]{1,0:T(8,128)(2,1)S(1)} %add_convert_fusion.1), channel_id=1, source_target_pairs={{0,1},{1,2},{2,3},{3,0},{4,5},{5,6},{6,7},{7,4},{8,9},{9,10},{10,1... | collective-permute-start | bytes 786440 | tf_op jit(solution)/shard_map/forward/ppermute | solution.py:126
  103.5 49.0 %collective-permute-start.15 = (bf16[128,1024]{1,0:T(8,128)(2,1)S(1)}, bf16[128,1024]{1,0:T(8,128)(2,1)}, u32[]{:S(2)}, u32[]{:S(2)}) collective-permute-start(bf16[128,1024]{1,0:T(8,128)(2,1)S(1)} %get-tuple-element.136), channel_id=1, source_target_pairs={{0,1},{1,2},{2,3},{3,0},{4,5},{5,6},{6,7},{7,4},{8,9},{9,10},{10,1... | collective-permute-start | bytes 786440 | tf_op jit(solution)/shard_map/rows/ppermute | solution.py:126
  104.2 48.4 %collective-permute-start.16 = (bf16[128,1024]{1,0:T(8,128)(2,1)S(1)}, bf16[128,1024]{1,0:T(8,128)(2,1)}, u32[]{:S(2)}, u32[]{:S(2)}) collective-permute-start(bf16[128,1024]{1,0:T(8,128)(2,1)S(1)} %get-tuple-element.136), channel_id=1, source_target_pairs={{0,2},{1,3},{2,0},{3,1},{4,6},{5,7},{6,4},{7,5},{8,10},{9,11},{10,... | collective-permute-start | bytes 786440 | tf_op jit(solution)/shard_map/rows/ppermute | solution.py:126
  111.2 41.4 %collective-permute-start.17 = (bf16[128,1024]{1,0:T(8,128)(2,1)S(1)}, bf16[128,1024]{1,0:T(8,128)(2,1)}, u32[]{:S(2)}, u32[]{:S(2)}) collective-permute-start(bf16[128,1024]{1,0:T(8,128)(2,1)S(1)} %get-tuple-element.136), channel_id=1, source_target_pairs={{0,3},{1,0},{2,1},{3,2},{4,7},{5,4},{6,5},{7,6},{8,11},{9,8},{10,9... | collective-permute-start | bytes 786440 | tf_op jit(solution)/shard_map/rows/ppermute | solution.py:126
  157.8 9.3 %collective-permute-start.18 = (bf16[128,1024]{1,0:T(8,128)(2,1)S(1)}, bf16[128,1024]{1,0:T(8,128)(2,1)S(1)}, u32[]{:S(2)}, u32[]{:S(2)}) collective-permute-start(bf16[128,1024]{1,0:T(8,128)(2,1)S(1)} %get-tuple-element.156), channel_id=1, source_target_pairs={{0,3},{1,0},{2,1},{3,2},{4,7},{5,4},{6,5},{7,6},{8,11},{9,8},{10,9... | collective-permute-start | bytes 786440 | tf_op jit(solution)/shard_map/branch/ppermute | solution.py:136
  157.9 14.1 %collective-permute-start.19 = (bf16[128,1024]{1,0:T(8,128)(2,1)S(1)}, bf16[128,1024]{1,0:T(8,128)(2,1)S(1)}, u32[]{:S(2)}, u32[]{:S(2)}) collective-permute-start(bf16[128,1024]{1,0:T(8,128)(2,1)S(1)} %get-tuple-element.158), channel_id=1, source_target_pairs={{0,2},{1,3},{2,0},{3,1},{4,6},{5,7},{6,4},{7,5},{8,10},{9,11},{10,... | collective-permute-start | bytes 786440 | tf_op jit(solution)/shard_map/branch/ppermute | solution.py:136
  159.4 12.7 %collective-permute-start.20 = (bf16[128,1024]{1,0:T(8,128)(2,1)S(1)}, bf16[128,1024]{1,0:T(8,128)(2,1)S(1)}, u32[]{:S(2)}, u32[]{:S(2)}) collective-permute-start(bf16[128,1024]{1,0:T(8,128)(2,1)S(1)} %get-tuple-element.157), channel_id=1, source_target_pairs={{0,1},{1,2},{2,3},{3,0},{4,5},{5,6},{6,7},{7,4},{8,9},{9,10},{10,1... | collective-permute-start | bytes 786440 | tf_op jit(solution)/shard_map/branch/ppermute | solution.py:136
  182.7 6.7 %collective-permute-start.12 = (bf16[128,1024]{1,0:T(8,128)(2,1)S(1)}, bf16[128,1024]{1,0:T(8,128)(2,1)S(1)}, u32[]{:S(2)}, u32[]{:S(2)}) collective-permute-start(bf16[128,1024]{1,0:T(8,128)(2,1)S(1)} %get-tuple-element.159), channel_id=1, source_target_pairs={{0,3},{1,0},{2,1},{3,2},{4,7},{5,4},{6,5},{7,6},{8,11},{9,8},{10,9... | collective-permute-start | bytes 786440 | tf_op jit(solution)/shard_map/result/ppermute | solution.py:136
  182.8 12.3 %collective-permute-start.13 = (bf16[128,1024]{1,0:T(8,128)(2,1)S(1)}, bf16[128,1024]{1,0:T(8,128)(2,1)S(1)}, u32[]{:S(2)}, u32[]{:S(2)}) collective-permute-start(bf16[128,1024]{1,0:T(8,128)(2,1)S(1)} %get-tuple-element.161), channel_id=1, source_target_pairs={{0,2},{1,3},{2,0},{3,1},{4,6},{5,7},{6,4},{7,5},{8,10},{9,11},{10,... | collective-permute-start | bytes 786440 | tf_op jit(solution)/shard_map/result/ppermute | solution.py:136
  183.4 12.7 %collective-permute-start.14 = (bf16[128,1024]{1,0:T(8,128)(2,1)S(1)}, bf16[128,1024]{1,0:T(8,128)(2,1)S(1)}, u32[]{:S(2)}, u32[]{:S(2)}) collective-permute-start(bf16[128,1024]{1,0:T(8,128)(2,1)S(1)} %get-tuple-element.160), channel_id=1, source_target_pairs={{0,1},{1,2},{2,3},{3,0},{4,5},{5,6},{6,7},{7,4},{8,9},{9,10},{10,1... | collective-permute-start | bytes 786440 | tf_op jit(solution)/shard_map/result/ppermute | solution.py:136
  198.3 8.3 %collective-permute-start.21 = (bf16[128,1024]{1,0:T(8,128)(2,1)}, bf16[128,1024]{1,0:T(8,128)(2,1)S(1)}, u32[]{:S(2)}, u32[]{:S(2)}) collective-permute-start(bf16[128,1024]{1,0:T(8,128)(2,1)} %get-tuple-element.138), channel_id=1, source_target_pairs={{0,1},{1,2},{2,3},{3,0},{4,5},{5,6},{6,7},{7,4},{8,9},{9,10},{10,1... | collective-permute-start | bytes 786440 | tf_op jit(solution)/shard_map/backward/ppermute | solution.py:126
  198.3 9.4 %collective-permute-start.22 = (bf16[128,1024]{1,0:T(8,128)(2,1)}, bf16[128,1024]{1,0:T(8,128)(2,1)S(1)}, u32[]{:S(2)}, u32[]{:S(2)}) collective-permute-start(bf16[128,1024]{1,0:T(8,128)(2,1)} %get-tuple-element.138), channel_id=1, source_target_pairs={{0,2},{1,3},{2,0},{3,1},{4,6},{5,7},{6,4},{7,5},{8,10},{9,11},{10,... | collective-permute-start | bytes 786440 | tf_op jit(solution)/shard_map/backward/ppermute | solution.py:126
  199.8 12.0 %collective-permute-start.23 = (bf16[128,1024]{1,0:T(8,128)(2,1)}, bf16[128,1024]{1,0:T(8,128)(2,1)S(1)}, u32[]{:S(2)}, u32[]{:S(2)}) collective-permute-start(bf16[128,1024]{1,0:T(8,128)(2,1)} %get-tuple-element.138), channel_id=1, source_target_pairs={{0,3},{1,0},{2,1},{3,2},{4,7},{5,4},{6,5},{7,6},{8,11},{9,8},{10,9... | collective-permute-start | bytes 786440 | tf_op jit(solution)/shard_map/backward/ppermute | solution.py:126
  223.0 8.9 %collective-permute-start.24 = (bf16[128,1024]{1,0:T(8,128)(2,1)S(1)}, bf16[128,1024]{1,0:T(8,128)(2,1)S(1)}, u32[]{:S(2)}, u32[]{:S(2)}) collective-permute-start(bf16[128,1024]{1,0:T(8,128)(2,1)S(1)} %get-tuple-element.153), channel_id=1, source_target_pairs={{0,3},{1,0},{2,1},{3,2},{4,7},{5,4},{6,5},{7,6},{8,11},{9,8},{10,9... | collective-permute-start | bytes 786440 | tf_op jit(solution)/shard_map/backward/ppermute | solution.py:136
  225.2 12.8 %collective-permute-start.25 = (bf16[128,1024]{1,0:T(8,128)(2,1)S(1)}, bf16[128,1024]{1,0:T(8,128)(2,1)S(1)}, u32[]{:S(2)}, u32[]{:S(2)}) collective-permute-start(bf16[128,1024]{1,0:T(8,128)(2,1)S(1)} %get-tuple-element.155), channel_id=1, source_target_pairs={{0,2},{1,3},{2,0},{3,1},{4,6},{5,7},{6,4},{7,5},{8,10},{9,11},{10,... | collective-permute-start | bytes 786440 | tf_op jit(solution)/shard_map/backward/ppermute | solution.py:136
  225.8 12.3 %collective-permute-start.26 = (bf16[128,1024]{1,0:T(8,128)(2,1)S(1)}, bf16[128,1024]{1,0:T(8,128)(2,1)S(1)}, u32[]{:S(2)}, u32[]{:S(2)}) collective-permute-start(bf16[128,1024]{1,0:T(8,128)(2,1)S(1)} %get-tuple-element.154), channel_id=1, source_target_pairs={{0,1},{1,2},{2,3},{3,0},{4,5},{5,6},{6,7},{7,4},{8,9},{9,10},{10,1... | collective-permute-start | bytes 786440 | tf_op jit(solution)/shard_map/backward/ppermute | solution.py:136
  269.6 13.1 %all-to-all-start.3 = ((bf16[4,32,2048]{2,1,0:T(8,128)(2,1)}), bf16[4,32,2048]{2,1,0:T(8,128)(2,1)}, u32[]{:S(2)}, u32[]{:S(2)}) async-start(bf16[4,32,2048]{2,1,0:T(8,128)(2,1)} %bitcast.150), calls=%async_computation.3 | async-start | bytes 1048576 | tf_op jit(solution)/shard_map/owners/all_to_all | solution.py:141
  273.7 73.6 %reduce-scatter.9.cloned.1.call-start = ((), (), s32[]{:S(2)}) async-start(), calls=%async_computation.9 | async-start | bytes 2654208 | tf_op jit(solution)/shard_map/attention_sums/reduce_scatter | solution.py:310
  347.3 9.8 %all-to-all-start.2 = ((bf16[4,32,1152]{2,1,0:T(8,128)(2,1)}), bf16[4,32,1152]{2,1,0:T(8,128)(2,1)S(1)}, u32[]{:S(2)}, u32[]{:S(2)}) async-start(bf16[4,32,1152]{2,1,0:T(8,128)(2,1)} %bitcast.157), calls=%async_computation.2 | async-start | bytes 589824 | tf_op jit(solution)/shard_map/owners/all_to_all | solution.py:141
  (38 other events, 299.7 us)
Sparse Core Ops, SparseCore 0:
  21.3 54.0 all-gather.2
  77.6 71.6 all-gather.4
  179.0 86.4 reduce-scatter.6
  278.2 69.1 reduce-scatter.8
